TPU v7x, 256 devices: a whole 4x4x8 slice. The times are simulated.
256 devices in a mesh: lon: 32 (over z, x_lo, core), lat: 8 (over x_hi, y).
Axes of the slice: x: 4 (x_hi: 2, x_lo: 2; x = x_hi * 2 + x_lo), y: 4, z: 8, core: 2. Of those that a mesh axis runs over, the one named last changes fastest.
Arguments:
- tracer: float32 [2, 2, 2048, 4096], P(None, None, 'lat', 'lon'), may hold values from -6 to 6
- transport: float32 [2, 2, 2048, 4096], P(None, None, 'lat', 'lon'), may hold values from -0.15 to 0.15
- diffusion: float32 [2, 2048, 4096], P(None, 'lat', 'lon'), may hold values from 0.01 to 0.06
- inverse_volume: float32 [2048, 4096], P('lat', 'lon'), may hold values from 0.5 to 2
- sea_mask: int32 [2048, 4096], P('lat', 'lon'), may hold values from 0 to 1, as said below
- regime: int32 [2, 2048, 4096], P(None, 'lat', 'lon'), may hold values from 0 to 2
Outputs:
- tracer_next: float32 [2, 2, 2048, 4096], P(None, None, 'lat', 'lon')
Inputs may be any that keep to these rules, and one draw needn't show every extreme that they name: `sea_mask`: the lowest 256 // 2 rows of the grid are land; above them about one cell in eight is land.
All inputs are finite; a program needn't handle non-finite values.
Results may differ from a plain program's by a relative error of at most 0.0003.
Values sent between devices are 32-bit elements; how exact they have to be, the bound alone decides.
A program may use at most 64 MiB of HBM per device.

v0:
```python
import jax
import jax.numpy as jnp
from jax import lax
from jax.sharding import PartitionSpec as P

STEPS = 2


def padded(cells, sides, width, closed):
    for axis, dim in sides:
        count = lax.axis_size(axis)
        ends = count if closed else count - 1
        head = lax.slice_in_dim(cells, 0, width, axis=dim)
        tail = lax.slice_in_dim(cells, cells.shape[dim] - width, cells.shape[dim], axis=dim)
        cells = jnp.concatenate(
            [
                lax.ppermute(tail, axis, [(i, (i + 1) % count) for i in range(ends)]),
                cells,
                lax.ppermute(head, axis, [((i + 1) % count, i) for i in range(ends)]),
            ],
            axis=dim,
        )
    return cells


def shifted(array, axis, by):
    devices = lax.axis_size(axis)
    return lax.ppermute(array, axis, [(i, (i + by) % devices) for i in range(devices)])


def from_behind(array, axis, by):
    devices = lax.axis_size(axis)
    pairs = [(i, i + by) for i in range(devices) if 0 <= i + by < devices]
    return lax.ppermute(array, axis, pairs)


def minmod(former, latter):
    smaller = jnp.where(jnp.abs(former) < jnp.abs(latter), former, latter)
    return jnp.where(former * latter > 0.0, smaller, jnp.zeros_like(smaller))


def face_flux(behind, current, following, beyond, velocity, regime_face, conduct, opened):
    plus_side = current + 0.5 * minmod(following - current, current - behind)
    minus_side = following + 0.5 * minmod(current - following, following - beyond)
    forward = velocity > 0.0
    limited = jnp.where(forward, plus_side, minus_side)
    upwind = jnp.where(forward, current, following)
    centred = 0.5 * (current + following)
    value = jnp.where(regime_face == 0, upwind, jnp.where(regime_face == 1, centred, limited))
    return opened * (velocity * value - conduct * (following - current))


def local(tracer, transport, diffusion, inverse_volume, sea_mask, regime):
    ocean = sea_mask.astype(jnp.float32)
    tracer_count, level_count, row_count, column_count = tracer.shape
    channels = tracer_count * level_count
    lat_index = lax.axis_index("lat")
    at_top = lat_index == lax.axis_size("lat") - 1
    lon_count = lax.axis_size("lon")

    def mirror_of(top_rows):
        width = top_rows.shape[2]
        gathered = lax.all_gather(top_rows, "lon", axis=2, tiled=True)
        mirror_start = (lon_count - 1 - lax.axis_index("lon")) * width
        mirror_rows = lax.dynamic_slice_in_dim(gathered, mirror_start, width, 2)
        return mirror_rows

    def extend(fields):
        top_rows = jnp.stack(
            [fields[:, row_count - 1, ::-1], fields[:, row_count - 2, ::-1]], axis=1
        )
        mirror_rows = mirror_of(top_rows)
        lat_ext = padded(fields, (("lat", 1),), 2, False)
        lon_ext = padded(fields, (("lon", 2),), 2, True)
        north_rows = jnp.where(at_top, mirror_rows, lat_ext[:, row_count + 2 :])
        lat_ext = jnp.concatenate([lat_ext[:, : row_count + 2], north_rows], axis=1)
        return (lat_ext, lon_ext)

    def fluxes(lon_ext, lat_ext, lon_mask, lat_mask):
        east = face_flux(
            lon_ext[..., 1 : column_count + 1],
            lon_ext[..., 2 : column_count + 2],
            lon_ext[..., 3 : column_count + 3],
            lon_ext[..., 4 : column_count + 4],
            transport[0],
            regime[0],
            diffusion[0],
            lon_mask[:, 2 : column_count + 2] * lon_mask[:, 3 : column_count + 3],
        )
        north = face_flux(
            lat_ext[..., 1 : row_count + 1, :],
            lat_ext[..., 2 : row_count + 2, :],
            lat_ext[..., 3 : row_count + 3, :],
            lat_ext[..., 4 : row_count + 4, :],
            transport[1],
            regime[1],
            diffusion[1],
            lat_mask[2 : row_count + 2, :] * lat_mask[3 : row_count + 3, :],
        )
        return (east, north)

    def tendency(field, masks):
        masked = field * ocean
        flattened = masked.reshape(channels, row_count, column_count)
        if masks is None:
            packed = jnp.concatenate([flattened, ocean[None]], axis=0)
            lat_all, lon_all = extend(packed)
            lat_mask = lat_all[channels]
            lon_mask = lon_all[channels]
            lat_all = lat_all[:channels]
            lon_all = lon_all[:channels]
        else:
            lat_mask, lon_mask = masks
            lat_all, lon_all = extend(flattened)
        lat_ext = lat_all.reshape(tracer_count, level_count, row_count + 4, column_count)
        lon_ext = lon_all.reshape(tracer_count, level_count, row_count, column_count + 4)
        east, north = fluxes(lon_ext, lat_ext, lon_mask, lat_mask)
        west_edge = shifted(east[..., -1], "lon", 1)
        west = jnp.concatenate([west_edge[..., None], east[..., :-1]], axis=-1)
        south_edge = from_behind(north[..., -1, :], "lat", 1)
        south = jnp.concatenate([south_edge[..., None, :], north[..., :-1, :]], axis=-2)
        return (inverse_volume * (west - east + (south - north)), (lat_mask, lon_mask))

    field = tracer
    masks = None
    for step_index in range(STEPS):
        masked = field * ocean
        change, masks = tendency(masked, masks)
        predictor = ocean * (masked + change)
        change, masks = tendency(predictor, masks)
        field = ocean * (0.5 * (masked + predictor) + 0.5 * change)
    return field


def solution(mesh):
    placed = (
        P(None, None, "lat", "lon"),
        P(None, None, "lat", "lon"),
        P(None, "lat", "lon"),
        P("lat", "lon"),
        P("lat", "lon"),
        P(None, "lat", "lon"),
    )
    return jax.shard_map(
        local, mesh=mesh, in_specs=placed, out_specs=P(None, None, "lat", "lon"), check_vma=False
    )
```

profile of v0, /device:TPU:4, one launch (start us, length us, event | category | flops | bytes accessed | tf_op | source)
XLA Modules:
  0.0 378.4 jit_solution(11049555554469972962)
XLA Ops:
  0.0 1.0 copy.78
  1.1 1.1 multiply_multiply_fusion
  2.4 0.9 pad_maximum_fusion.18
  3.4 4.9 %collective-permute-start.3 = (f32[5,2,128]{1,2,0:T(8,128)}, f32[5,2,128]{1,2,0:T(8,128)}, u32[]{:S(2)}, u32[]{:S(2)}) collective-permute-start(f32[5,2,128]{1,2,0:T(8,128)} %get-tuple-element.18), channel_id=1, source_target_pairs={{1,0},{2,1},{3,2},{4,3},{5,4},{6,5},{7,6},{9,8},{10,9},{11,10},{12... | collective-permute-start | bytes 15368 | tf_op jit(solution)/shard_map/ppermute | solution.py:19
  8.2 1.9 collective-permute-start.4
  10.2 6.6 %collective-permute-start.1 = (f32[5,256,2]{1,2,0:T(2,128)S(1)}, f32[5,256,2]{1,2,0:T(2,128)S(1)}, u32[]{:S(2)}, u32[]{:S(2)}) collective-permute-start(f32[5,256,2]{1,2,0:T(2,128)S(1)} %get-tuple-element.16), channel_id=1, source_target_pairs={{8,0},{16,8},{24,16},{32,24},{40,32},{48,40},{56,48},{64,56},{72,6... | collective-permute-start | bytes 30728 | tf_op jit(solution)/shard_map/ppermute | solution.py:19
  17.0 1.1 slice_bitcast_fusion.1
  18.1 1.1 broadcast_compare_fusion.1
  19.5 1.0 slice_bitcast_fusion.3
  20.5 1.7 compare_bitcast_fusion.3
  22.4 124.3 %all_gather.12 = f32[5,2,4096]{1,2,0:T(8,128)} all-gather(f32[5,2,128]{1,2,0:T(8,128)S(1)} %pad_maximum_fusion.19), channel_id=1, replica_groups=mesh['lon'=32,'lat'=8] {'lon'}, dimensions={2}, use_global_device_ids=true | all-gather | bytes 168960 | tf_op jit(solution)/shard_map/all_gather | solution.py:63
  146.7 1.1 dynamic-slice_select_fusion
  147.8 1.3 pad_maximum_fusion
  149.1 1.6 fusion.54
  151.4 2.0 copy.105
  153.4 1.0 copy.107
  154.4 2.1 copy.104
  156.5 1.0 copy.106
  157.7 1.2 fusion.55
  158.9 1.2 copy.101
  160.2 2.1 copy.103
  162.2 2.0 copy.100
  164.3 1.0 copy.102
  166.1 2.0 subtract_multiply_fusion.11
  168.9 2.1 subtract_multiply_fusion.9
  171.1 1.9 collective-permute-start.5
  173.0 0.7 collective-permute-done.2
  173.7 1.0 copy.86
  174.7 5.4 %collective-permute-done.5 = f32[2,2,128]{2,1,0:T(2,128)S(1)} collective-permute-done((f32[2,2,128]{2,1,0:T(2,128)S(1)}, f32[2,2,128]{2,1,0:T(2,128)S(1)}, u32[]{:S(2)}, u32[]{:S(2)}) %collective-permute-start.5) | collective-permute-done | bytes 2080 | tf_op jit(solution)/shard_map/ppermute | solution.py:34
  180.2 2.1 broadcast_multiply_fusion.1
  182.5 2.0 collective-permute-start.9
  184.7 33.4 %all_gather.13 = f32[4,2,4096]{2,1,0:T(2,128)S(1)} all-gather(f32[4,2,128]{2,1,0:T(2,128)S(1)} %pad_maximum_fusion.24), channel_id=1, replica_groups=mesh['lon'=32,'lat'=8] {'lon'}, dimensions={2}, use_global_device_ids=true | all-gather | bytes 135168 | tf_op jit(solution)/shard_map/all_gather | solution.py:63
  218.1 1.9 collective-permute-start.10
  220.0 1.0 collective-permute-start.6
  221.0 6.7 %collective-permute-done.6 = f32[4,256,2]{2,1,0:T(8,128)S(1)} collective-permute-done((f32[4,256,2]{2,1,0:T(8,128)S(1)}, f32[4,256,2]{2,1,0:T(8,128)S(1)}, u32[]{:S(2)}, u32[]{:S(2)}) %collective-permute-start.6) | collective-permute-done | bytes 8224 | tf_op jit(solution)/shard_map/ppermute | solution.py:19
  227.7 4.1 %collective-permute-done.7 = f32[4,256,2]{2,1,0:T(8,128)S(1)} collective-permute-done((f32[4,256,2]{2,1,0:T(8,128)S(1)}, f32[4,256,2]{2,1,0:T(8,128)S(1)}, u32[]{:S(2)}, u32[]{:S(2)}) %collective-permute-start.7) | collective-permute-done | bytes 8224 | tf_op jit(solution)/shard_map/ppermute | solution.py:17
  231.8 1.7 subtract_multiply_fusion.7
  233.9 3.0 collective-permute-start.8
  236.9 1.5 subtract_multiply_fusion.6
  238.5 1.9 collective-permute-start.11
  240.4 1.7 copy.95
  242.1 1.0 copy.93
  243.1 4.5 %collective-permute-done.11 = f32[2,2,128]{2,1,0:T(2,128)S(1)} collective-permute-done((f32[2,2,128]{2,1,0:T(2,128)S(1)}, f32[2,2,128]{2,1,0:T(2,128)S(1)}, u32[]{:S(2)}, u32[]{:S(2)}) %collective-permute-start.11) | collective-permute-done | bytes 2080 | tf_op jit(solution)/shard_map/ppermute | solution.py:34
  247.6 1.6 broadcast_multiply_fusion
  249.4 3.6 collective-permute-start.15
  253.3 31.8 %all_gather.14 = f32[4,2,4096]{2,1,0:T(2,128)S(1)} all-gather(f32[4,2,128]{2,1,0:T(2,128)S(1)} %pad_maximum_fusion.25), channel_id=1, replica_groups=mesh['lon'=32,'lat'=8] {'lon'}, dimensions={2}, use_global_device_ids=true | all-gather | bytes 135168 | tf_op jit(solution)/shard_map/all_gather | solution.py:63
  285.1 2.7 collective-permute-start.16
  288.4 6.3 %collective-permute-done.12 = f32[4,256,2]{2,1,0:T(8,128)S(1)} collective-permute-done((f32[4,256,2]{2,1,0:T(8,128)S(1)}, f32[4,256,2]{2,1,0:T(8,128)S(1)}, u32[]{:S(2)}, u32[]{:S(2)}) %collective-permute-start.12) | collective-permute-done | bytes 8224 | tf_op jit(solution)/shard_map/ppermute | solution.py:19
  294.7 4.1 %collective-permute-done.13 = f32[4,256,2]{2,1,0:T(8,128)S(1)} collective-permute-done((f32[4,256,2]{2,1,0:T(8,128)S(1)}, f32[4,256,2]{2,1,0:T(8,128)S(1)}, u32[]{:S(2)}, u32[]{:S(2)}) %collective-permute-start.13) | collective-permute-done | bytes 8224 | tf_op jit(solution)/shard_map/ppermute | solution.py:17
  298.8 1.9 subtract_multiply_fusion.4
  301.1 3.5 collective-permute-start.14
  304.6 1.5 subtract_multiply_fusion.3
  306.1 2.2 collective-permute-start.17
  308.6 6.6 %collective-permute-done.17 = f32[2,2,128]{2,1,0:T(2,128)S(1)} collective-permute-done((f32[2,2,128]{2,1,0:T(2,128)S(1)}, f32[2,2,128]{2,1,0:T(2,128)S(1)}, u32[]{:S(2)}, u32[]{:S(2)}) %collective-permute-start.17) | collective-permute-done | bytes 2080 | tf_op jit(solution)/shard_map/ppermute | solution.py:34
  315.2 2.0 broadcast_multiply_fusion.2
  318.0 3.1 collective-permute-start.21
  321.3 35.1 %all_gather.15 = f32[4,2,4096]{2,1,0:T(2,128)S(1)} all-gather(f32[4,2,128]{2,1,0:T(2,128)S(1)} %pad_maximum_fusion.26), channel_id=1, replica_groups=mesh['lon'=32,'lat'=8] {'lon'}, dimensions={2}, use_global_device_ids=true | all-gather | bytes 135168 | tf_op jit(solution)/shard_map/all_gather | solution.py:63
  356.4 1.9 collective-permute-start.22
  358.4 2.0 subtract_multiply_fusion.1
  361.1 4.5 %collective-permute-done.22 = f32[4,2,128]{2,1,0:T(2,128)S(1)} collective-permute-done((f32[4,2,128]{2,1,0:T(2,128)S(1)}, f32[4,2,128]{2,1,0:T(2,128)S(1)}, u32[]{:S(2)}, u32[]{:S(2)}) %collective-permute-start.22) | collective-permute-done | bytes 4128 | tf_op jit(solution)/shard_map/ppermute | solution.py:17
  365.5 1.5 subtract_multiply_fusion
  367.1 1.9 collective-permute-start.23
  369.2 6.9 %collective-permute-done.23 = f32[2,2,128]{2,1,0:T(2,128)S(1)} collective-permute-done((f32[2,2,128]{2,1,0:T(2,128)S(1)}, f32[2,2,128]{2,1,0:T(2,128)S(1)}, u32[]{:S(2)}, u32[]{:S(2)}) %collective-permute-start.23) | collective-permute-done | bytes 2080 | tf_op jit(solution)/shard_map/ppermute | solution.py:34
  376.2 2.2 fusion.34
  (81 shorter events, 7.8 us)
Async XLA Ops:
  3.4 143.3 %collective-permute-start.3 = (f32[5,2,128]{1,2,0:T(8,128)}, f32[5,2,128]{1,2,0:T(8,128)}, u32[]{:S(2)}, u32[]{:S(2)}) collective-permute-start(f32[5,2,128]{1,2,0:T(8,128)} %get-tuple-element.18), channel_id=1, source_target_pairs={{1,0},{2,1},{3,2},{4,3},{5,4},{6,5},{7,6},{9,8},{10,9},{11,10},{12... | collective-permute-start | bytes 15368 | tf_op jit(solution)/shard_map/ppermute | solution.py:19
  8.2 139.6 %collective-permute-start.4 = (f32[5,2,128]{1,2,0:T(8,128)}, f32[5,2,128]{1,2,0:T(8,128)}, u32[]{:S(2)}, u32[]{:S(2)}) collective-permute-start(f32[5,2,128]{1,2,0:T(8,128)} %get-tuple-element.17), channel_id=1, source_target_pairs={{0,1},{1,2},{2,3},{3,4},{4,5},{5,6},{6,7},{8,9},{9,10},{10,11},{11... | collective-permute-start | bytes 15368 | tf_op jit(solution)/shard_map/ppermute | solution.py:17
  10.2 147.5 %collective-permute-start.1 = (f32[5,256,2]{1,2,0:T(2,128)S(1)}, f32[5,256,2]{1,2,0:T(2,128)S(1)}, u32[]{:S(2)}, u32[]{:S(2)}) collective-permute-start(f32[5,256,2]{1,2,0:T(2,128)S(1)} %get-tuple-element.16), channel_id=1, source_target_pairs={{8,0},{16,8},{24,16},{32,24},{40,32},{48,40},{56,48},{64,56},{72,6... | collective-permute-start | bytes 30728 | tf_op jit(solution)/shard_map/ppermute | solution.py:19
  16.8 140.9 %collective-permute-start = (f32[5,256,2]{1,2,0:T(2,128)S(1)}, f32[5,256,2]{1,2,0:T(2,128)S(1)}, u32[]{:S(2)}, u32[]{:S(2)}) collective-permute-start(f32[5,256,2]{1,2,0:T(2,128)S(1)} %get-tuple-element.15), channel_id=1, source_target_pairs={{0,8},{8,16},{16,24},{24,32},{32,40},{40,48},{48,56},{56,64},{64,7... | collective-permute-start | bytes 30728 | tf_op jit(solution)/shard_map/ppermute | solution.py:17
  19.2 149.7 %copy-start.5 = (pred[2,256,128]{2,1,0:T(8,128)(4,1)}, pred[2,256,128]{2,1,0:T(8,128)(4,1)S(1)}, u32[]{:S(2)}) copy-start(pred[2,256,128]{2,1,0:T(8,128)(4,1)S(1)} %get-tuple-element.44) | copy-start | bytes 196612
  19.2 212.6 %copy-start.4 = (pred[2,256,128]{2,1,0:T(8,128)(4,1)}, pred[2,256,128]{2,1,0:T(8,128)(4,1)S(1)}, u32[]{:S(2)}) copy-start(pred[2,256,128]{2,1,0:T(8,128)(4,1)S(1)} %get-tuple-element.43) | copy-start | bytes 196612
  20.5 211.3 %copy-start.2 = (f32[256,128]{1,0:T(8,128)}, f32[256,128]{1,0:T(8,128)S(1)}, u32[]{:S(2)}) copy-start(f32[256,128]{1,0:T(8,128)S(1)} %get-tuple-element.51) | copy-start | bytes 393220
  154.4 25.8 %copy-start = (f32[2,2,256,128]{3,2,1,0:T(8,128)S(1)}, f32[2,2,256,128]{3,2,1,0:T(8,128)}, u32[]{:S(2)}) copy-start(f32[2,2,256,128]{3,2,1,0:T(8,128)} %param.6) | copy-start | bytes 1572868
  154.4 25.8 %copy-start.3 = (f32[256,128]{1,0:T(8,128)S(1)}, f32[256,128]{1,0:T(8,128)}, u32[]{:S(2)}) copy-start(f32[256,128]{1,0:T(8,128)} %param.9) | copy-start | bytes 393220
  157.6 1.3 copy-start.6
  166.1 70.9 %copy-start.1 = (f32[256,128]{1,0:T(8,128)}, f32[256,128]{1,0:T(8,128)S(1)}, u32[]{:S(2)}) copy-start(f32[256,128]{1,0:T(8,128)S(1)} %copy.81) | copy-start | bytes 393220
  168.5 5.2 %collective-permute-start.2 = (f32[2,2,256]{2,1,0:T(2,128)S(1)}, f32[2,2,256]{2,1,0:T(2,128)S(1)}, u32[]{:S(2)}, u32[]{:S(2)}) collective-permute-start(f32[2,2,256]{2,1,0:T(2,128)S(1)} %slice_reduce_fusion.3), channel_id=1, source_target_pairs={{0,8},{8,16},{16,24},{24,32},{32,40},{40,48},{48,56},{56,64},{64,7... | collective-permute-start | bytes 12296 | tf_op jit(solution)/shard_map/ppermute | solution.py:28
  171.1 9.1 %collective-permute-start.5 = (f32[2,2,128]{2,1,0:T(2,128)S(1)}, f32[2,2,128]{2,1,0:T(2,128)S(1)}, u32[]{:S(2)}, u32[]{:S(2)}) collective-permute-start(f32[2,2,128]{2,1,0:T(2,128)S(1)} %bitcast.120), channel_id=1, source_target_pairs={{0,1},{1,2},{2,3},{3,4},{4,5},{5,6},{6,7},{8,9},{9,10},{10,11},{11... | collective-permute-start | bytes 6152 | tf_op jit(solution)/shard_map/ppermute | solution.py:34
  182.5 38.5 %collective-permute-start.9 = (f32[4,2,128]{2,1,0:T(2,128)S(1)}, f32[4,2,128]{2,1,0:T(2,128)S(1)}, u32[]{:S(2)}, u32[]{:S(2)}) collective-permute-start(f32[4,2,128]{2,1,0:T(2,128)S(1)} %get-tuple-element.40), channel_id=1, source_target_pairs={{1,0},{2,1},{3,2},{4,3},{5,4},{6,5},{7,6},{9,8},{10,9},{11,10},{12... | collective-permute-start | bytes 12296 | tf_op jit(solution)/shard_map/ppermute | solution.py:19
  218.1 18.9 %collective-permute-start.10 = (f32[4,2,128]{2,1,0:T(2,128)S(1)}, f32[4,2,128]{2,1,0:T(2,128)S(1)}, u32[]{:S(2)}, u32[]{:S(2)}) collective-permute-start(f32[4,2,128]{2,1,0:T(2,128)S(1)} %get-tuple-element.39), channel_id=1, source_target_pairs={{0,1},{1,2},{2,3},{3,4},{4,5},{5,6},{6,7},{8,9},{9,10},{10,11},{11... | collective-permute-start | bytes 12296 | tf_op jit(solution)/shard_map/ppermute | solution.py:17
  220.0 7.8 %collective-permute-start.6 = (f32[4,256,2]{2,1,0:T(8,128)S(1)}, f32[4,256,2]{2,1,0:T(8,128)S(1)}, u32[]{:S(2)}, u32[]{:S(2)}) collective-permute-start(f32[4,256,2]{2,1,0:T(8,128)S(1)} %get-tuple-element.38), channel_id=1, source_target_pairs={{8,0},{16,8},{24,16},{32,24},{40,32},{48,40},{56,48},{64,56},{72,6... | collective-permute-start | bytes 24584 | tf_op jit(solution)/shard_map/ppermute | solution.py:19
  221.0 10.8 %collective-permute-start.7 = (f32[4,256,2]{2,1,0:T(8,128)S(1)}, f32[4,256,2]{2,1,0:T(8,128)S(1)}, u32[]{:S(2)}, u32[]{:S(2)}) collective-permute-start(f32[4,256,2]{2,1,0:T(8,128)S(1)} %get-tuple-element.37), channel_id=1, source_target_pairs={{0,8},{8,16},{16,24},{24,32},{32,40},{40,48},{48,56},{56,64},{64,7... | collective-permute-start | bytes 24584 | tf_op jit(solution)/shard_map/ppermute | solution.py:17
  233.9 8.2 %collective-permute-start.8 = (f32[2,2,256]{2,1,0:T(2,128)S(1)}, f32[2,2,256]{2,1,0:T(2,128)S(1)}, u32[]{:S(2)}, u32[]{:S(2)}) collective-permute-start(f32[2,2,256]{2,1,0:T(2,128)S(1)} %slice_reduce_fusion.2), channel_id=1, source_target_pairs={{0,8},{8,16},{16,24},{24,32},{32,40},{40,48},{48,56},{56,64},{64,7... | collective-permute-start | bytes 12296 | tf_op jit(solution)/shard_map/ppermute | solution.py:28
  238.5 9.1 %collective-permute-start.11 = (f32[2,2,128]{2,1,0:T(2,128)S(1)}, f32[2,2,128]{2,1,0:T(2,128)S(1)}, u32[]{:S(2)}, u32[]{:S(2)}) collective-permute-start(f32[2,2,128]{2,1,0:T(2,128)S(1)} %bitcast.119), channel_id=1, source_target_pairs={{0,1},{1,2},{2,3},{3,4},{4,5},{5,6},{6,7},{8,9},{9,10},{10,11},{11... | collective-permute-start | bytes 6152 | tf_op jit(solution)/shard_map/ppermute | solution.py:34
  249.4 39.0 %collective-permute-start.15 = (f32[4,2,128]{2,1,0:T(2,128)S(1)}, f32[4,2,128]{2,1,0:T(2,128)S(1)}, u32[]{:S(2)}, u32[]{:S(2)}) collective-permute-start(f32[4,2,128]{2,1,0:T(2,128)S(1)} %get-tuple-element.34), channel_id=1, source_target_pairs={{1,0},{2,1},{3,2},{4,3},{5,4},{6,5},{7,6},{9,8},{10,9},{11,10},{12... | collective-permute-start | bytes 12296 | tf_op jit(solution)/shard_map/ppermute | solution.py:19
  285.1 19.5 %collective-permute-start.16 = (f32[4,2,128]{2,1,0:T(2,128)S(1)}, f32[4,2,128]{2,1,0:T(2,128)S(1)}, u32[]{:S(2)}, u32[]{:S(2)}) collective-permute-start(f32[4,2,128]{2,1,0:T(2,128)S(1)} %get-tuple-element.33), channel_id=1, source_target_pairs={{0,1},{1,2},{2,3},{3,4},{4,5},{5,6},{6,7},{8,9},{9,10},{10,11},{11... | collective-permute-start | bytes 12296 | tf_op jit(solution)/shard_map/ppermute | solution.py:17
  287.8 6.9 %collective-permute-start.12 = (f32[4,256,2]{2,1,0:T(8,128)S(1)}, f32[4,256,2]{2,1,0:T(8,128)S(1)}, u32[]{:S(2)}, u32[]{:S(2)}) collective-permute-start(f32[4,256,2]{2,1,0:T(8,128)S(1)} %get-tuple-element.32), channel_id=1, source_target_pairs={{8,0},{16,8},{24,16},{32,24},{40,32},{48,40},{56,48},{64,56},{72,6... | collective-permute-start | bytes 24584 | tf_op jit(solution)/shard_map/ppermute | solution.py:19
  288.0 10.9 %collective-permute-start.13 = (f32[4,256,2]{2,1,0:T(8,128)S(1)}, f32[4,256,2]{2,1,0:T(8,128)S(1)}, u32[]{:S(2)}, u32[]{:S(2)}) collective-permute-start(f32[4,256,2]{2,1,0:T(8,128)S(1)} %get-tuple-element.31), channel_id=1, source_target_pairs={{0,8},{8,16},{16,24},{24,32},{32,40},{40,48},{48,56},{56,64},{64,7... | collective-permute-start | bytes 24584 | tf_op jit(solution)/shard_map/ppermute | solution.py:17
  301.1 7.2 %collective-permute-start.14 = (f32[2,2,256]{2,1,0:T(2,128)S(1)}, f32[2,2,256]{2,1,0:T(2,128)S(1)}, u32[]{:S(2)}, u32[]{:S(2)}) collective-permute-start(f32[2,2,256]{2,1,0:T(2,128)S(1)} %slice_reduce_fusion.1), channel_id=1, source_target_pairs={{0,8},{8,16},{16,24},{24,32},{32,40},{40,48},{48,56},{56,64},{64,7... | collective-permute-start | bytes 12296 | tf_op jit(solution)/shard_map/ppermute | solution.py:28
  306.1 9.1 %collective-permute-start.17 = (f32[2,2,128]{2,1,0:T(2,128)S(1)}, f32[2,2,128]{2,1,0:T(2,128)S(1)}, u32[]{:S(2)}, u32[]{:S(2)}) collective-permute-start(f32[2,2,128]{2,1,0:T(2,128)S(1)} %bitcast.121), channel_id=1, source_target_pairs={{0,1},{1,2},{2,3},{3,4},{4,5},{5,6},{6,7},{8,9},{9,10},{10,11},{11... | collective-permute-start | bytes 6152 | tf_op jit(solution)/shard_map/ppermute | solution.py:34
  317.4 41.0 %collective-permute-start.18 = (f32[4,256,2]{2,1,0:T(8,128)S(1)}, f32[4,256,2]{2,1,0:T(8,128)S(1)}, u32[]{:S(2)}, u32[]{:S(2)}) collective-permute-start(f32[4,256,2]{2,1,0:T(8,128)S(1)} %get-tuple-element.30), channel_id=1, source_target_pairs={{8,0},{16,8},{24,16},{32,24},{40,32},{48,40},{56,48},{64,56},{72,6... | collective-permute-start | bytes 24584 | tf_op jit(solution)/shard_map/ppermute | solution.py:19
  317.5 40.9 %collective-permute-start.19 = (f32[4,256,2]{2,1,0:T(8,128)S(1)}, f32[4,256,2]{2,1,0:T(8,128)}, u32[]{:S(2)}, u32[]{:S(2)}) collective-permute-start(f32[4,256,2]{2,1,0:T(8,128)S(1)} %get-tuple-element.29), channel_id=1, source_target_pairs={{0,8},{8,16},{16,24},{24,32},{32,40},{40,48},{48,56},{56,64},{64,7... | collective-permute-start | bytes 24584 | tf_op jit(solution)/shard_map/ppermute | solution.py:17
  318.0 40.4 %collective-permute-start.21 = (f32[4,2,128]{2,1,0:T(2,128)S(1)}, f32[4,2,128]{2,1,0:T(2,128)S(1)}, u32[]{:S(2)}, u32[]{:S(2)}) collective-permute-start(f32[4,2,128]{2,1,0:T(2,128)S(1)} %get-tuple-element.26), channel_id=1, source_target_pairs={{1,0},{2,1},{3,2},{4,3},{5,4},{6,5},{7,6},{9,8},{10,9},{11,10},{12... | collective-permute-start | bytes 12296 | tf_op jit(solution)/shard_map/ppermute | solution.py:19
  356.4 9.1 %collective-permute-start.22 = (f32[4,2,128]{2,1,0:T(2,128)S(1)}, f32[4,2,128]{2,1,0:T(2,128)S(1)}, u32[]{:S(2)}, u32[]{:S(2)}) collective-permute-start(f32[4,2,128]{2,1,0:T(2,128)S(1)} %get-tuple-element.25), channel_id=1, source_target_pairs={{0,1},{1,2},{2,3},{3,4},{4,5},{5,6},{6,7},{8,9},{9,10},{10,11},{11... | collective-permute-start | bytes 12296 | tf_op jit(solution)/shard_map/ppermute | solution.py:17
  360.8 8.2 %collective-permute-start.20 = (f32[2,2,256]{2,1,0:T(2,128)S(1)}, f32[2,2,256]{2,1,0:T(2,128)S(1)}, u32[]{:S(2)}, u32[]{:S(2)}) collective-permute-start(f32[2,2,256]{2,1,0:T(2,128)S(1)} %slice_reduce_fusion), channel_id=1, source_target_pairs={{0,8},{8,16},{16,24},{24,32},{32,40},{40,48},{48,56},{56,64},{64,7... | collective-permute-start | bytes 12296 | tf_op jit(solution)/shard_map/ppermute | solution.py:28
  367.1 9.1 %collective-permute-start.23 = (f32[2,2,128]{2,1,0:T(2,128)S(1)}, f32[2,2,128]{2,1,0:T(2,128)S(1)}, u32[]{:S(2)}, u32[]{:S(2)}) collective-permute-start(f32[2,2,128]{2,1,0:T(2,128)S(1)} %bitcast.122), channel_id=1, source_target_pairs={{0,1},{1,2},{2,3},{3,4},{4,5},{5,6},{6,7},{8,9},{9,10},{10,11},{11... | collective-permute-start | bytes 6152 | tf_op jit(solution)/shard_map/ppermute | solution.py:34
where the time goes:
time: 381 us; the launch traced here: 378 us
  blocking collectives  225 us (59%)
  waiting for transfers between devices  49.9 us (13%)
  starting transfers between devices  46 us (12%)
  other arithmetic  31.4 us (8%)
  local copies, waits for them, and re-layouts  26 us (7%)
    all_gather x4, blocking collectives, mirror_of(): gathered = lax.all_gather(top_rows, 'lon', axis=2, tiled=True)  225 us
    ppermute x4, waiting for transfers between devices, from_behind(): return lax.ppermute(array, axis, pairs)  23.5 us
    ppermute x8, starting transfers between devices, padded(): lax.ppermute(head, axis, [((i + 1) % count, i) for i in range(ends)])  21.4 us
    mul x8, other arithmetic, face_flux(): return opened * (velocity * value - conduct * (following - current))  14.3 us
    unnamed x23, local copies, waits for them, and re-layouts  13.5 us
    ppermute x8, waiting for transfers between devices, padded(): lax.ppermute(head, axis, [((i + 1) % count, i) for i in range(ends)])  13 us
    ppermute x8, waiting for transfers between devices, padded(): lax.ppermute(tail, axis, [(i, (i + 1) % count) for i in range(ends)])  12.7 us
    ppermute x8, starting transfers between devices, padded(): lax.ppermute(tail, axis, [(i, (i + 1) % count) for i in range(ends)])  9.45 us
  transfers between devices with their start and end apart: 24, of which 10 were waited for; matrix products, arithmetic and copies ran while one was open for 9% of the time, Pallas kernels for 0%

commit v1 on v0

v1 whole, which is shorter than its diff:
```python
import functools

import jax
import jax.numpy as jnp
from jax import lax
from jax.experimental import pallas as pl
from jax.experimental.pallas import tpu as pltpu
from jax.sharding import PartitionSpec as P

STEPS = 2
MESH = pl.DeviceIdType.MESH
HALO = 8
ROWS = 256
LANES = 128
CHANNELS = 4
F32 = jnp.float32

EAST, NORTH = 0, 3


def iota(rows, axis):
    return lax.broadcasted_iota(jnp.int32, (rows, LANES), axis)


def lanes(tile, index):
    return jnp.take_along_axis(tile, index, axis=1, mode="promise_in_bounds")


def sublanes(tile, index):
    return jnp.take_along_axis(tile, index, axis=0, mode="promise_in_bounds")


def lanes_of(rows, index):
    tiles = [lanes(rows[8 * i : 8 * i + 8], index) for i in range(rows.shape[0] // 8)]
    return tiles[0] if len(tiles) == 1 else jnp.concatenate(tiles, axis=0)


def face_flux(cell, gap, gap_behind, gap_beyond, a, b, c):
    other = jnp.where(a > 0.0, gap_behind, gap_beyond)
    slope = jnp.maximum(jnp.minimum(gap, 0.0), jnp.minimum(other, jnp.maximum(gap, 0.0)))
    return a * cell + b * gap + c * slope


def face_coefficients(velocity, conduct, regime, opened):
    a = opened * velocity
    share = jnp.where(regime == 1.0, 0.5, jnp.where(velocity > 0.0, 0.0, 1.0))
    b = a * share - opened * conduct
    c = jnp.where(regime == 2.0, 0.5 * jnp.abs(a), 0.0)
    return a, b, c


def stage(source, target, kept, planes, north_flux, start, count, channels, levels):
    volume = planes[6 * levels, pl.ds(start, count)]
    for ch in range(channels):
        level = 6 * (ch % levels)

        def plane(i):
            return planes[level + i, pl.ds(start, count)]

        cell = source[ch, pl.ds(start, count)]
        behind = source[ch, pl.ds(start - 1, count)]
        ahead = source[ch, pl.ds(start + 1, count)]
        beyond = source[ch, pl.ds(start + 2, count)]
        north = face_flux(
            cell, ahead - cell, cell - behind, beyond - ahead, plane(3), plane(4), plane(5)
        )
        north_flux[ch, pl.ds(start, count)] = north
        gap = pltpu.roll(cell, LANES - 1, 1) - cell
        east = face_flux(
            cell,
            gap,
            pltpu.roll(gap, 1, 1),
            pltpu.roll(gap, LANES - 1, 1),
            plane(0),
            plane(1),
            plane(2),
        )
        west = pltpu.roll(east, 1, 1)
        south = north_flux[ch, pl.ds(start - 1, count)]
        change = volume * ((west - east) + (south - north))
        if kept is None:
            target[ch, pl.ds(start, count)] = cell + change
        else:
            target[ch, pl.ds(start, count)] = 0.5 * ((kept[ch, pl.ds(start, count)] + cell) + change)


def fold_fix(source, target, planes, second, row, channels, levels, factor):
    first_row = iota(8, 0) == 0
    for ch in range(channels):
        level = 6 * (ch % levels)
        extra = 3 * (ch % levels)
        cell = source[ch, pl.ds(row - 1, 8)]
        behind = source[ch, pl.ds(row - 2, 8)]
        ahead = source[ch, pl.ds(row, 8)]
        beyond = source[ch, pl.ds(row + 1, 8)]
        gaps = (cell, ahead - cell, cell - behind, beyond - ahead)
        mine = face_flux(*gaps, *[planes[level + 3 + i, pl.ds(row - 1, 8)] for i in range(3)])
        theirs = face_flux(*gaps, *[second[extra + i] for i in range(3)])
        volume = planes[6 * levels, pl.ds(row, 8)]
        fix = jnp.where(first_row, volume * (theirs - mine), 0.0)
        target[ch, pl.ds(row, 8)] = target[ch, pl.ds(row, 8)] + factor * fix


def kernel(
    lon_count,
    lat_count,
    tracer,
    transport,
    diffusion,
    inverse_volume,
    sea_mask,
    regime,
    out,
    in_tracer,
    in_transport,
    in_diffusion,
    in_volume,
    in_mask,
    in_regime,
    far_tracer,
    far_transport,
    far_diffusion,
    far_volume,
    far_mask,
    far_regime,
    mask,
    field,
    guess,
    planes,
    flux,
    packs,
    edges,
    lat_mask,
    lat_field,
    lat_guess,
    lat_planes,
    lat_flux,
    lat_up,
    lat_second,
    lon_raw,
    lon_field,
    lon_guess,
    lon_planes,
    lon_flux,
    lon_second_raw,
    lon_second,
    load_sem,
    lat_send,
    lat_recv,
    lon_send,
    lon_recv,
    corner_send,
    corner_recv,
):
    lon = lax.axis_index("lon")
    lat = lax.axis_index("lat")
    top = lat == lat_count - 1
    bottom = lat == 0
    left = lax.rem(lon + lon_count - 1, lon_count)
    right = lax.rem(lon + 1, lon_count)
    up = jnp.where(top, lat, lat + 1)
    up_lon = jnp.where(top, lon_count - 1 - lon, lon)
    up_left = jnp.where(top, lax.rem(lon_count - lon, lon_count), left)
    up_right = jnp.where(top, lax.rem(2 * lon_count - 2 - lon, lon_count), right)
    self_left = jnp.logical_and(top, up_left == lon)
    self_right = jnp.logical_and(top, up_right == lon)
    down = jnp.where(bottom, lat, lat - 1)

    barrier = pltpu.get_barrier_semaphore()

    def greet(to_lon, to_lat):
        pl.semaphore_signal(
            barrier, inc=1, device_id={"lon": to_lon, "lat": to_lat}, device_id_type=MESH
        )

    greet(left, lat)
    greet(right, lat)
    greet(up_lon, up)

    @pl.when(jnp.logical_not(self_left))
    def _():
        greet(up_left, up)

    @pl.when(jnp.logical_not(self_right))
    def _():
        greet(up_right, up)

    @pl.when(jnp.logical_not(bottom))
    def _():
        greet(lon, down)
        greet(left, down)
        greet(right, down)

    arrays = (tracer, transport, diffusion, inverse_volume, sea_mask, regime)
    held = (in_tracer, in_transport, in_diffusion, in_volume, in_mask, in_regime)
    landing = (far_tracer, far_transport, far_diffusion, far_volume, far_mask, far_regime)
    loads = [pltpu.make_async_copy(a, h, load_sem.at[i]) for i, (a, h) in enumerate(zip(arrays, held))]
    for load in loads:
        load.start()

    pad = jnp.zeros((8, LANES), F32)
    for ref, last in ((field, ROWS), (guess, ROWS), (flux, ROWS), (planes, ROWS)):
        for i in range(ref.shape[0]):
            ref[i, pl.ds(0, 8)] = pad
            ref[i, pl.ds(8 + last, 8)] = pad
    mask[pl.ds(ROWS + 8, 8)] = pad
    for ref, last in ((lat_field, 48), (lat_guess, 48), (lat_flux, 48)):
        for i in range(ref.shape[0]):
            ref[i, pl.ds(0, 8)] = pad
            ref[i, pl.ds(8 + last, 8)] = pad
    for ref in (lon_field, lon_guess, lon_flux):
        for i in range(2):
            ref[i, 0, pl.ds(0, 8)] = pad
            ref[i, 0, pl.ds(8 + ROWS + 16, 8)] = pad
    lat_mask[pl.ds(56, 8)] = pad
    for i in range(2):
        lon_raw[i, 6, pl.ds(ROWS + 16, 8)] = pad

    @pl.when(bottom)
    def _():
        for ref in landing:
            ref[0] = jnp.zeros(ref.shape[1:], ref.dtype)
        for i in range(2):
            edges[i, pl.ds(0, 8)] = pad

    for load in loads:
        load.wait()

    def pack(i, carry):
        n = 64
        r = pl.multiple_of(i * n, n)
        rows, padded = pl.ds(r, n), pl.ds(pl.multiple_of(r + 8, 8), n)
        group = iota(n, 1) >> 3
        sea = in_mask[rows].astype(F32)
        mask[padded] = sea
        volume = in_volume[rows] * sea
        planes[12, padded] = volume
        cells = []
        for ch in range(CHANNELS):
            cell = in_tracer[ch // 2, ch % 2, rows] * sea
            field[ch, padded] = cell
            cells.append(cell)
        cells += [in_transport[j // 2, j % 2, rows] for j in range(4)]
        cells += [in_diffusion[j, rows] for j in range(2)]
        cells += [volume, sea]
        cells += [in_regime[j, rows].astype(F32) for j in range(2)]
        west_pack = east_pack = cells[0]
        for k in range(1, 14):
            moved = pltpu.roll(cells[k], 8 * k, 1)
            west_pack = jnp.where(group == k, moved, west_pack)
            east_pack = jnp.where(group == k - 1, moved, east_pack)
        east_pack = jnp.where(group == 15, cells[0], east_pack)
        packs[0, rows] = west_pack
        packs[1, rows] = east_pack
        return carry

    lax.fori_loop(0, 4, pack, 0)

    pl.semaphore_wait(
        barrier,
        5
        - self_left.astype(jnp.int32)
        - self_right.astype(jnp.int32)
        + 3 * jnp.logical_not(bottom).astype(jnp.int32),
    )

    def remote(src, dst, send, recv, to_lon, to_lat):
        return pltpu.make_async_remote_copy(
            src_ref=src,
            dst_ref=dst,
            send_sem=send,
            recv_sem=recv,
            device_id={"lon": to_lon, "lat": to_lat},
            device_id_type=MESH,
        )

    def row_slice(ref, start):
        return ref.at[(slice(None),) * (len(ref.shape) - 2) + (pl.ds(start, 8),)]

    to_left = remote(packs.at[0], edges.at[1, pl.ds(8, ROWS)], lon_send.at[0], lon_recv.at[1], left, lat)
    to_right = remote(packs.at[1], edges.at[0, pl.ds(8, ROWS)], lon_send.at[1], lon_recv.at[0], right, lat)
    corner_row = pl.multiple_of(jnp.where(top, ROWS + 8, 0), 8)
    top_int = top.astype(jnp.int32)
    corner_ul = remote(
        packs.at[0, pl.ds(ROWS - 8, 8)],
        edges.at[1 - top_int, pl.ds(corner_row, 8)],
        corner_send.at[0],
        corner_recv.at[1 + top_int],
        up_left,
        up,
    )
    corner_ur = remote(
        packs.at[1, pl.ds(ROWS - 8, 8)],
        edges.at[top_int, pl.ds(corner_row, 8)],
        corner_send.at[1],
        corner_recv.at[3 * top_int],
        up_right,
        up,
    )
    corner_dl = remote(
        packs.at[0, pl.ds(0, 8)],
        edges.at[1, pl.ds(ROWS + 8, 8)],
        corner_send.at[2],
        corner_recv.at[3],
        left,
        down,
    )
    corner_dr = remote(
        packs.at[1, pl.ds(0, 8)],
        edges.at[0, pl.ds(ROWS + 8, 8)],
        corner_send.at[3],
        corner_recv.at[2],
        right,
        down,
    )
    to_up = [
        remote(row_slice(a, ROWS - 8), f.at[top_int], lat_send.at[0, i], lat_recv.at[top_int, i], up_lon, up)
        for i, (a, f) in enumerate(zip(arrays, landing))
    ]
    to_down = [
        remote(row_slice(a, 0), f.at[1], lat_send.at[1, i], lat_recv.at[1, i], lon, down)
        for i, (a, f) in enumerate(zip(arrays, landing))
    ]
    to_left.start()
    to_right.start()

    @pl.when(jnp.logical_not(self_left))
    def _():
        corner_ul.start()

    @pl.when(jnp.logical_not(self_right))
    def _():
        corner_ur.start()

    for copy in to_up:
        copy.start()

    @pl.when(jnp.logical_not(bottom))
    def _():
        corner_dl.start()
        corner_dr.start()
        for copy in to_down:
            copy.start()

    @pl.when(self_left)
    def _():
        edges[0, pl.ds(ROWS + 8, 8)] = packs[0, pl.ds(ROWS - 8, 8)]

    @pl.when(self_right)
    def _():
        edges[1, pl.ds(ROWS + 8, 8)] = packs[1, pl.ds(ROWS - 8, 8)]

    lane, row8 = iota(8, 1), iota(8, 0)
    slot, place = lane >> 5, lane & 31
    odd = slot & 1
    own_index = (jnp.maximum(place - 8, 0), jnp.minimum(place + 104, LANES - 1))
    own_lane = (place >= 8, place < 24)
    pack_slot = [slot, 4 + odd, 6 + odd] + [jnp.full_like(slot, k) for k in range(8, 14)]

    def unpack_index(side, a):
        at = pack_slot[a] if side == 1 else (pack_slot[a] + 15) & 15
        return 8 * at + (lane & 7)

    def own_strips(side, fourteen):
        index = own_index[side]
        n = fourteen[0].shape[0]
        wide_slot, wide_odd = iota(n, 1) >> 5, (iota(n, 1) >> 5) & 1
        got = [lanes_of(a, index) for a in fourteen]
        cell = got[0]
        for ch in range(1, CHANNELS):
            cell = jnp.where(wide_slot == ch, got[ch], cell)
        speed_east = jnp.where(wide_odd == 1, got[5], got[4])
        speed_north = jnp.where(wide_odd == 1, got[7], got[6])
        return [cell, speed_east, speed_north] + got[8:]

    def prepare(i, carry):
        n = 64
        r = pl.multiple_of(i * n, n)
        rows, padded = pl.ds(r, n), pl.ds(pl.multiple_of(r + 8, 8), n)
        sea = mask[padded]
        open_east = sea * pltpu.roll(sea, LANES - 1, 1)
        open_north = sea * mask[pl.ds(r + 9, n)]
        regimes = [in_regime[j, rows].astype(F32) for j in range(2)]
        for level in range(2):
            for way, opened in ((0, open_east), (1, open_north)):
                found = face_coefficients(
                    in_transport[way, level, rows], in_diffusion[way, rows], regimes[way], opened
                )
                for j in range(3):
                    planes[6 * level + 3 * way + j, padded] = found[j]
        return carry

    lax.fori_loop(0, 4, prepare, 0)

    def strips(i, carry):
        n = 32
        r = pl.multiple_of(i * n, n)
        rows, padded = pl.ds(r, n), pl.ds(pl.multiple_of(r + 8, 8), n)
        fourteen = [field[ch, padded] for ch in range(CHANNELS)]
        fourteen += [in_transport[j // 2, j % 2, rows] for j in range(4)]
        fourteen += [in_diffusion[j, rows] for j in range(2)]
        fourteen += [planes[12, padded], mask[padded]]
        fourteen += [in_regime[j, rows].astype(F32) for j in range(2)]
        for side in range(2):
            for a, strip in enumerate(own_strips(side, fourteen)):
                lon_raw[side, a, padded] = strip
        return carry

    lax.fori_loop(0, 8, strips, 0)

    for ch in range(CHANNELS):
        lat_field[ch, pl.ds(16, 16)] = field[ch, pl.ds(8, 16)]
        lat_field[ch, pl.ds(32, 16)] = field[ch, pl.ds(ROWS - 8, 16)]
    for i in range(13):
        lat_planes[i, pl.ds(16, 16)] = planes[i, pl.ds(8, 16)]
        lat_planes[i, pl.ds(32, 16)] = planes[i, pl.ds(ROWS - 8, 16)]
    lat_mask[pl.ds(16, 16)] = mask[pl.ds(8, 16)]
    lat_mask[pl.ds(32, 16)] = mask[pl.ds(ROWS - 8, 16)]

    def interior(step, carry):
        def predict(i, c):
            stage(field, guess, None, planes, flux, pl.multiple_of(i * 32 + 8, 8), 32, CHANNELS, 2)
            return c

        def correct(i, c):
            stage(guess, field, field, planes, flux, pl.multiple_of(i * 32 + 8, 8), 32, CHANNELS, 2)
            return c

        lax.fori_loop(0, 8, predict, 0)
        lax.fori_loop(0, 8, correct, 0)
        return carry

    lax.fori_loop(0, STEPS, interior, 0)

    for i, f in enumerate(landing):
        remote(f.at[1], f.at[1], lat_send.at[0, i], lat_recv.at[1, i], lon, lat).wait_recv()

    @pl.when(jnp.logical_not(bottom))
    def _():
        for i, f in enumerate(landing):
            remote(f.at[0], f.at[0], lat_send.at[0, i], lat_recv.at[0, i], lon, lat).wait_recv()
        for side in range(2):
            remote(
                edges.at[side, pl.ds(0, 8)], edges.at[side, pl.ds(0, 8)], corner_send.at[0],
                corner_recv.at[side], lon, lat,
            ).wait_recv()

    @pl.when(jnp.logical_not(self_left))
    def _():
        remote(
            edges.at[0, pl.ds(ROWS + 8, 8)], edges.at[0, pl.ds(ROWS + 8, 8)], corner_send.at[0],
            corner_recv.at[2], lon, lat,
        ).wait_recv()

    @pl.when(jnp.logical_not(self_right))
    def _():
        remote(
            edges.at[1, pl.ds(ROWS + 8, 8)], edges.at[1, pl.ds(ROWS + 8, 8)], corner_send.at[0],
            corner_recv.at[3], lon, lat,
        ).wait_recv()

    def prepared(side):
        sea = far_mask[side].astype(F32)
        tiles = [far_tracer[side, ch // 2, ch % 2] * sea for ch in range(CHANNELS)]
        tiles += [far_transport[side, j // 2, j % 2] for j in range(4)]
        tiles += [far_diffusion[side, j] for j in range(2)]
        tiles += [far_volume[side] * sea, sea]
        tiles += [far_regime[side, j].astype(F32) for j in range(2)]
        return tiles

    below = prepared(0)
    for side in range(2):
        for a, strip in enumerate(own_strips(side, below)):
            lon_raw[side, a, pl.ds(0, 8)] = strip

    @pl.when(jnp.logical_not(top))
    def _():
        above = prepared(1)
        for k, tile in enumerate(above):
            lat_up[k] = tile
        for side in range(2):
            for a, strip in enumerate(own_strips(side, above)):
                lon_raw[side, a, pl.ds(ROWS + 8, 8)] = strip

    row_cell, row_north = 7 - row8, jnp.maximum(6 - row8, 0)

    @pl.when(top)
    def _():
        across = prepared(1)
        lane_cell, lane_east = LANES - 1 - lane, jnp.maximum(LANES - 2 - lane, 0)
        for k, tile in enumerate(across):
            east, north = k in (4, 5, 8, 12), k in (6, 7, 9, 13)
            turned = lanes(tile, lane_east if east else lane_cell)
            if k in (4, 5, 6, 7):
                turned = -turned
            lat_up[k] = sublanes(turned, row_north if north else row_cell)
            if north:
                lat_up[14 + (6, 7, 9, 13).index(k)] = sublanes(turned, row_cell)
        slot_cell, slot_east = lane ^ 31, 32 * slot + jnp.maximum(30 - place, 0)
        for side in range(2):
            whole = own_strips(1 - side, across)
            corner = edges[side, pl.ds(ROWS + 8, 8)]
            for a, strip in enumerate(whole):
                strip = jnp.where(own_lane[1 - side], strip, lanes(corner, unpack_index(1 - side, a)))
                east, north = a in (1, 3, 7), a in (2, 4, 8)
                turned = lanes(strip, slot_east if east else slot_cell)
                if a in (1, 2):
                    turned = -turned
                lon_raw[side, a, pl.ds(ROWS + 8, 8)] = sublanes(turned, row_north if north else row_cell)
                if north:
                    lon_second_raw[side, (2, 4, 8).index(a)] = sublanes(turned, row_cell)

    lat_mask[pl.ds(8, 8)] = below[11]
    lat_mask[pl.ds(48, 8)] = lat_up[11]
    for ch in range(CHANNELS):
        lat_field[ch, pl.ds(8, 8)] = below[ch]
        lat_field[ch, pl.ds(48, 8)] = lat_up[ch]
    lat_planes[12, pl.ds(8, 8)] = below[10]
    lat_planes[12, pl.ds(48, 8)] = lat_up[10]
    highest = [None] * 4 + [in_transport[j // 2, j % 2, pl.ds(ROWS - 8, 8)] for j in range(4)]
    highest += [in_diffusion[j, pl.ds(ROWS - 8, 8)] for j in range(2)] + [None, None]
    highest += [in_regime[j, pl.ds(ROWS - 8, 8)].astype(F32) for j in range(2)]
    upper = [lat_up[k] for k in range(14)]
    for at, tiles in ((8, below), (40, highest), (48, upper)):
        sea = lat_mask[pl.ds(at, 8)]
        opened = (sea * pltpu.roll(sea, LANES - 1, 1), sea * lat_mask[pl.ds(at + 1, 8)])
        for level in range(2):
            for way in range(2):
                found = face_coefficients(
                    tiles[4 + 2 * way + level], tiles[8 + way], tiles[12 + way], opened[way]
                )
                for j in range(3):
                    lat_planes[6 * level + 3 * way + j, pl.ds(at, 8)] = found[j]

    for side in range(2):
        remote(
            edges.at[side, pl.ds(8, ROWS)], edges.at[side, pl.ds(8, ROWS)], lon_send.at[0],
            lon_recv.at[side], lon, lat,
        ).wait_recv()

    def join(i, carry):
        n = 136
        r = pl.multiple_of(i * n, 8)
        rows, padded = pl.ds(r, n), pl.ds(pl.multiple_of(r + 8, 8), n)
        wide_place = iota(n, 1) & 31
        whole = jnp.logical_and(iota(n, 0) + r >= ROWS + 8, top)
        for side in range(2):
            own = jnp.logical_or(wide_place >= 8 if side == 0 else wide_place < 24, whole)
            edge = edges[side, rows]
            for a in range(9):
                strip = jnp.where(own, lon_raw[side, a, rows], lanes_of(edge, unpack_index(side, a)))
                if a == 0:
                    lon_field[side, 0, padded] = strip
                elif a == 5:
                    lon_planes[side, 6, padded] = strip
                else:
                    lon_raw[side, a, rows] = strip
        return carry

    lax.fori_loop(0, 2, join, 0)

    def lon_coefficients(i, carry):
        n = 136
        r = pl.multiple_of(i * n, 8)
        rows, padded = pl.ds(r, n), pl.ds(pl.multiple_of(r + 8, 8), n)
        for side in range(2):
            sea = lon_raw[side, 6, rows]
            opened = (sea * pltpu.roll(sea, LANES - 1, 1), sea * lon_raw[side, 6, pl.ds(r + 1, n)])
            for way in range(2):
                found = face_coefficients(
                    lon_raw[side, 1 + way, rows],
                    lon_raw[side, 3 + way, rows],
                    lon_raw[side, 7 + way, rows],
                    opened[way],
                )
                for j in range(3):
                    lon_planes[side, 3 * way + j, padded] = found[j]
        return carry

    lax.fori_loop(0, 2, lon_coefficients, 0)

    @pl.when(top)
    def _():
        opened = lat_mask[pl.ds(47, 8)] * lat_mask[pl.ds(48, 8)]
        for level in range(2):
            found = face_coefficients(lat_up[14 + level], lat_up[16], lat_up[17], opened)
            for j in range(3):
                lat_second[3 * level + j] = found[j]
        for side in range(2):
            opened = lon_raw[side, 6, pl.ds(ROWS + 7, 8)] * lon_raw[side, 6, pl.ds(ROWS + 8, 8)]
            found = face_coefficients(*[lon_second_raw[side, j] for j in range(3)], opened)
            for j in range(3):
                lon_second[side, j] = found[j]

    def rim(step, carry):
        for source, target, kept, factor in ((0, 1, None, 1.0), (1, 0, 0, 0.5)):
            lat_pair = (lat_field, lat_guess)
            stage(
                lat_pair[source], lat_pair[target], None if kept is None else lat_field,
                lat_planes, lat_flux, 8, 48, CHANNELS, 2,
            )
            for side in range(2):
                pair = (lon_field.at[side], lon_guess.at[side])
                stage(
                    pair[source], pair[target], None if kept is None else pair[0],
                    lon_planes.at[side], lon_flux.at[side], 8, ROWS + 16, 1, 1,
                )

            @pl.when(top)
            def _():
                fold_fix(lat_pair[source], lat_pair[target], lat_planes, lat_second, 48, CHANNELS, 2, factor)
                for side in range(2):
                    pair = (lon_field.at[side], lon_guess.at[side])
                    fold_fix(
                        pair[source], pair[target], lon_planes.at[side], lon_second.at[side],
                        ROWS + 16, 1, 1, factor,
                    )

        return carry

    lax.fori_loop(0, STEPS, rim, 0)

    for ch in range(CHANNELS):
        field[ch, pl.ds(8, 8)] = lat_field[ch, pl.ds(16, 8)]
        field[ch, pl.ds(ROWS, 8)] = lat_field[ch, pl.ds(40, 8)]

    def finish(i, carry):
        n = 64
        r = pl.multiple_of(i * n, n)
        rows, padded = pl.ds(r, n), pl.ds(pl.multiple_of(r + 8, 8), n)
        deep = pl.ds(pl.multiple_of(r + 16, 8), n)
        wide = iota(n, 1)
        both = jnp.where((wide & 31) < 16, lon_field[0, 0, deep], lon_field[1, 0, deep])
        inner = jnp.logical_and(wide >= 8, wide < LANES - 8)
        for ch in range(CHANNELS):
            index = 32 * ch + (lane & 7) + jnp.where(lane < 64, 8, 16)
            out[ch // 2, ch % 2, rows] = jnp.where(inner, field[ch, padded], lanes_of(both, index))
        return carry

    lax.fori_loop(0, 4, finish, 0)

    to_left.wait_send()
    to_right.wait_send()
    for copy in to_up:
        copy.wait_send()

    @pl.when(jnp.logical_not(self_left))
    def _():
        corner_ul.wait_send()

    @pl.when(jnp.logical_not(self_right))
    def _():
        corner_ur.wait_send()

    @pl.when(jnp.logical_not(bottom))
    def _():
        corner_dl.wait_send()
        corner_dr.wait_send()
        for copy in to_down:
            copy.wait_send()


def solution(mesh):
    lon_count, lat_count = mesh.shape["lon"], mesh.shape["lat"]
    placed = (
        P(None, None, "lat", "lon"),
        P(None, None, "lat", "lon"),
        P(None, "lat", "lon"),
        P("lat", "lon"),
        P("lat", "lon"),
        P(None, "lat", "lon"),
    )

    def local(*arrays):
        shapes = [a.shape for a in arrays]
        types = [a.dtype for a in arrays]
        far = [(2,) + s[:-2] + (8, LANES) for s in shapes]
        tall, wide = ROWS + 16, ROWS + 32

        def vmem(*shape):
            return pltpu.VMEM(shape, F32)

        return pl.pallas_call(
            functools.partial(kernel, lon_count, lat_count),
            out_shape=pltpu.VMEM(shapes[0], F32),
            in_specs=[pl.BlockSpec(memory_space=pl.ANY)] * 6,
            out_specs=pl.BlockSpec(memory_space=pltpu.VMEM),
            scratch_shapes=[
                *[pltpu.VMEM(s, t) for s, t in zip(shapes, types)],
                *[pltpu.VMEM(s, t) for s, t in zip(far, types)],
                vmem(tall, LANES),
                vmem(CHANNELS, tall, LANES),
                vmem(CHANNELS, tall, LANES),
                vmem(13, tall, LANES),
                vmem(CHANNELS, tall, LANES),
                vmem(2, ROWS, LANES),
                vmem(2, tall, LANES),
                vmem(64, LANES),
                vmem(CHANNELS, 64, LANES),
                vmem(CHANNELS, 64, LANES),
                vmem(13, 64, LANES),
                vmem(CHANNELS, 64, LANES),
                vmem(18, 8, LANES),
                vmem(6, 8, LANES),
                vmem(2, 9, tall + 8, LANES),
                vmem(2, 1, wide, LANES),
                vmem(2, 1, wide, LANES),
                vmem(2, 7, wide, LANES),
                vmem(2, 1, wide, LANES),
                vmem(2, 3, 8, LANES),
                vmem(2, 3, 8, LANES),
                pltpu.SemaphoreType.DMA((6,)),
                pltpu.SemaphoreType.DMA((2, 6)),
                pltpu.SemaphoreType.DMA((2, 6)),
                pltpu.SemaphoreType.DMA((2,)),
                pltpu.SemaphoreType.DMA((2,)),
                pltpu.SemaphoreType.DMA((4,)),
                pltpu.SemaphoreType.DMA((4,)),
            ],
            compiler_params=pltpu.CompilerParams(
                collective_id=0, has_side_effects=True, vmem_limit_bytes=40 * 1024 * 1024
            ),
        )(*arrays)

    return jax.shard_map(
        local, mesh=mesh, in_specs=placed, out_specs=P(None, None, "lat", "lon"), check_vma=False
    )
```

time: 381 us -> 30 us (0.08)
  blocking collectives: 225 us -> 0 us
  waiting for transfers between devices: 49.9 us -> 0 us
  starting transfers between devices: 46 us -> 0 us
  other arithmetic: 31.4 us -> 0 us
  Pallas kernels: 0 us -> 23.1 us
  local copies, waits for them, and re-layouts: 26 us -> 6.58 us
    all_gather x4 -> x0, blocking collectives: 225 us -> none  [mirror_of(): gathered = lax.all_gather(top_rows, 'lon', axis=2, tiled=True)]
    ppermute x24 -> x0, waiting for transfers between devices: 49.9 us -> none  [the longest x4 23.5 us: from_behind(): return lax.ppermute(array, axis, pairs)]
    ppermute x24 -> x0, starting transfers between devices: 46 us -> none  [the longest x8 21.4 us: padded(): lax.ppermute(head, axis, [((i + 1) % count, i) for i in range(ends)])]
    mul x15 -> x0, other arithmetic: 24 us -> none  [the longest x8 14.3 us: face_flux(): return opened * (velocity * value - conduct * (following - current))]
    pallas_call x0 -> x1, Pallas kernels: none -> 23.1 us  [local(): pl.pallas_call(functools.partial(kernel, lon_count, lat_count), out_shape...]
    unnamed x23 -> x13, local copies, waits for them, and re-layouts: 13.5 us -> 6.58 us
    slice x19 -> x0, local copies, waits for them, and re-layouts: 4.97 us -> none  [the longest x1 1.56 us: fluxes(): lat_ext[..., 1:row_count + 1, :]]
    mul x6 -> x0, local copies, waits for them, and re-layouts: 4.09 us -> none  [the longest x2 2.06 us: face_flux(): return opened * (velocity * value - conduct * (following - current))]
  transfers between devices with their start and end apart: 24 -> 0, of which waited for: 10 -> 0; matrix products, arithmetic and copies ran while one was open for 9% -> 0% of each run, Pallas kernels for 0% -> 0%
where the time goes in v1:
time: 30 us; the launch traced here: 29.7 us
  Pallas kernels  23.1 us (77%)
  local copies, waits for them, and re-layouts  6.58 us (22%)
    pallas_call x1, Pallas kernels, local(): pl.pallas_call(functools.partial(kernel, lon_count, lat_count), out_shape...  23.1 us
    unnamed x13, local copies, waits for them, and re-layouts  6.58 us

profile of v1, /device:TPU:4, one launch (start us, length us, event | category | flops | bytes accessed | tf_op | source)
XLA Modules:
  0.0 29.7 jit_solution(11153253318289368735)
XLA Ops:
  0.0 0.0 copy-start
  0.0 1.0 %copy-done = f32[2,2,256,128]{3,2,1,0:T(8,128)S(1)} copy-done((f32[2,2,256,128]{3,2,1,0:T(8,128)S(1)}, f32[2,2,256,128]{3,2,1,0:T(8,128)}, u32[]{:S(2)}) %copy-start) | copy-done | bytes 524312
  1.0 0.0 copy-start.1
  1.0 1.0 %copy-done.1 = f32[2,2,256,128]{3,2,1,0:T(8,128)S(1)} copy-done((f32[2,2,256,128]{3,2,1,0:T(8,128)S(1)}, f32[2,2,256,128]{3,2,1,0:T(8,128)}, u32[]{:S(2)}) %copy-start.1) | copy-done | bytes 524312
  2.1 0.0 copy-start.2
  2.1 0.9 %copy-done.2 = f32[2,256,128]{2,1,0:T(8,128)S(1)} copy-done((f32[2,256,128]{2,1,0:T(8,128)S(1)}, f32[2,256,128]{2,1,0:T(8,128)}, u32[]{:S(2)}) %copy-start.2) | copy-done | bytes 262168
  3.0 0.0 copy-start.3
  3.0 0.9 %copy-done.3 = s32[2,256,128]{2,1,0:T(8,128)S(1)} copy-done((s32[2,256,128]{2,1,0:T(8,128)S(1)}, s32[2,256,128]{2,1,0:T(8,128)}, u32[]{:S(2)}) %copy-start.3) | copy-done | bytes 262168
  4.0 0.0 copy-start.4
  4.0 0.9 %copy-done.4 = f32[256,128]{1,0:T(8,128)S(1)} copy-done((f32[256,128]{1,0:T(8,128)S(1)}, f32[256,128]{1,0:T(8,128)}, u32[]{:S(2)}) %copy-start.4) | copy-done | bytes 131096
  4.9 0.0 copy-start.5
  4.9 0.9 %copy-done.5 = s32[256,128]{1,0:T(8,128)S(1)} copy-done((s32[256,128]{1,0:T(8,128)S(1)}, s32[256,128]{1,0:T(8,128)}, u32[]{:S(2)}) %copy-start.5) | copy-done | bytes 131096
  5.8 23.1 %shard_map.64 = f32[2,2,256,128]{3,2,1,0:T(8,128)S(1)} custom-call(f32[2,2,256,128]{3,2,1,0:T(8,128)S(1)} %copy-done, f32[2,2,256,128]{3,2,1,0:T(8,128)S(1)} %copy-done.1, f32[2,256,128]{2,1,0:T(8,128)S(1)} %copy-done.2, f32[256,128]{1,0:T(8,128)S(1)} %copy-done.4, s32[256,128]{1,0:T(8,128)S(1)} %copy-done.5, s32[2,256,128]{2,1,0:T(8,128)S(1)} %copy-done.3), custom_call_target="tpu_custom_call" | custom-call | tf_op jit(solution)/shard_map/pallas_call | solution.py:683
  28.9 0.8 %copy.8 = f32[2,2,256,128]{3,2,1,0:T(8,128)} copy(f32[2,2,256,128]{3,2,1,0:T(8,128)S(1)} %shard_map.64) | data formatting | bytes 1048576
Async XLA Ops:
  0.0 1.0 %copy-start = (f32[2,2,256,128]{3,2,1,0:T(8,128)S(1)}, f32[2,2,256,128]{3,2,1,0:T(8,128)}, u32[]{:S(2)}) copy-start(f32[2,2,256,128]{3,2,1,0:T(8,128)} %tracer.1) | copy-start | bytes 1572868
  1.0 1.0 %copy-start.1 = (f32[2,2,256,128]{3,2,1,0:T(8,128)S(1)}, f32[2,2,256,128]{3,2,1,0:T(8,128)}, u32[]{:S(2)}) copy-start(f32[2,2,256,128]{3,2,1,0:T(8,128)} %transport.1) | copy-start | bytes 1572868
  2.1 0.9 %copy-start.2 = (f32[2,256,128]{2,1,0:T(8,128)S(1)}, f32[2,256,128]{2,1,0:T(8,128)}, u32[]{:S(2)}) copy-start(f32[2,256,128]{2,1,0:T(8,128)} %diffusion.1) | copy-start | bytes 786436
  3.0 0.9 %copy-start.3 = (s32[2,256,128]{2,1,0:T(8,128)S(1)}, s32[2,256,128]{2,1,0:T(8,128)}, u32[]{:S(2)}) copy-start(s32[2,256,128]{2,1,0:T(8,128)} %regime.1) | copy-start | bytes 786436
  4.0 0.9 %copy-start.4 = (f32[256,128]{1,0:T(8,128)S(1)}, f32[256,128]{1,0:T(8,128)}, u32[]{:S(2)}) copy-start(f32[256,128]{1,0:T(8,128)} %inverse_volume.1) | copy-start | bytes 393220
  4.9 0.9 %copy-start.5 = (s32[256,128]{1,0:T(8,128)S(1)}, s32[256,128]{1,0:T(8,128)}, u32[]{:S(2)}) copy-start(s32[256,128]{1,0:T(8,128)} %sea_mask.1) | copy-start | bytes 393220

commit v2 on v1

v2 whole, which is shorter than its diff:
```python
import functools

import jax
import jax.numpy as jnp
from jax import lax
from jax.experimental import pallas as pl
from jax.experimental.pallas import tpu as pltpu
from jax.sharding import PartitionSpec as P

STEPS = 2
MESH = pl.DeviceIdType.MESH
HALO = 8
ROWS = 256
LANES = 128
CHANNELS = 4
F32 = jnp.float32
INNER = 256
PACK = 64
JOIN = 136

SENT = 13


def iota(rows, axis):
    return lax.broadcasted_iota(jnp.int32, (rows, LANES), axis)


def lanes(tile, index):
    return jnp.take_along_axis(tile, index, axis=1, mode="promise_in_bounds")


def sublanes(tile, index):
    return jnp.take_along_axis(tile, index, axis=0, mode="promise_in_bounds")


def lanes_of(rows, index):
    tiles = [lanes(rows[8 * i : 8 * i + 8], index) for i in range(rows.shape[0] // 8)]
    return tiles[0] if len(tiles) == 1 else jnp.concatenate(tiles, axis=0)


def face_flux(cell, gap, gap_behind, gap_beyond, a, b, c):
    other = jnp.where(a > 0.0, gap_behind, gap_beyond)
    slope = jnp.maximum(jnp.minimum(gap, 0.0), jnp.minimum(other, jnp.maximum(gap, 0.0)))
    return a * cell + b * gap + c * slope


def face_coefficients(velocity, conduct, regime, opened):
    a = opened * velocity
    share = jnp.where(regime == 1.0, 0.5, jnp.where(velocity > 0.0, 0.0, 1.0))
    b = a * share - opened * conduct
    c = jnp.where(regime == 2.0, 0.5 * jnp.abs(a), 0.0)
    return a, b, c


def stage(source, target, kept, planes, north_flux, start, count, channels, levels, fold=None, patch=None):
    rows = pl.ds(start, count)
    volume = planes[6 * levels, rows]
    results = []
    for ch in range(channels):
        level = 6 * (ch % levels)

        def plane(i):
            return planes[level + i, rows]

        cell = source[ch, rows]
        behind = source[ch, pl.ds(start - 1, count)]
        ahead = source[ch, pl.ds(start + 1, count)]
        beyond = source[ch, pl.ds(start + 2, count)]
        north = face_flux(
            cell, ahead - cell, cell - behind, beyond - ahead, plane(3), plane(4), plane(5)
        )
        north_flux[ch, rows] = north
        if fold is not None:
            second, row = fold
            at = [source[ch, pl.ds(row + i, 8)] for i in (-2, -1, 0, 1)]
            theirs = face_flux(
                at[1],
                at[2] - at[1],
                at[1] - at[0],
                at[3] - at[2],
                *[second[3 * (ch % levels) + i] for i in range(3)],
            )
            north_flux[ch, pl.ds(row - 1, 1)] = theirs[0:1]
        east1 = pltpu.roll(cell, LANES - 1, 1)
        east2 = pltpu.roll(cell, LANES - 2, 1)
        west1 = pltpu.roll(cell, 1, 1)
        east = face_flux(
            cell,
            east1 - cell,
            cell - west1,
            east2 - east1,
            plane(0),
            plane(1),
            plane(2),
        )
        west = pltpu.roll(east, 1, 1)
        south = north_flux[ch, pl.ds(start - 1, count)]
        result = volume * ((west - east) + (south - north))
        if kept is None:
            result = cell + result
        else:
            result = 0.5 * ((kept[ch, rows] + cell) + result)
        if patch is not None:
            result = patch(result)
        target[ch, rows] = result
        results.append(result)
    return results


def kernel(
    lon_count,
    lat_count,
    tracer,
    transport,
    diffusion,
    inverse_volume,
    sea_mask,
    regime,
    out,
    in_tracer,
    in_transport,
    in_diffusion,
    in_volume,
    in_mask,
    in_regime,
    mask,
    field,
    guess,
    planes,
    flux,
    packs,
    edges,
    lat_packs,
    lat_edges,
    lat_mask,
    lat_field,
    lat_guess,
    lat_planes,
    lat_flux,
    lat_up,
    lat_second,
    lon_raw,
    lon_field,
    lon_guess,
    lon_planes,
    lon_flux,
    lon_second,
    patches,
    load_sem,
    lat_send,
    lat_recv,
    lon_send,
    lon_recv,
    corner_send,
    corner_recv,
):
    lon = lax.axis_index("lon")
    lat = lax.axis_index("lat")
    top = lat == lat_count - 1
    bottom = lat == 0
    left = lax.rem(lon + lon_count - 1, lon_count)
    right = lax.rem(lon + 1, lon_count)
    up = jnp.where(top, lat, lat + 1)
    up_lon = jnp.where(top, lon_count - 1 - lon, lon)
    up_left = jnp.where(top, lax.rem(lon_count - lon, lon_count), left)
    up_right = jnp.where(top, lax.rem(2 * lon_count - 2 - lon, lon_count), right)
    self_left = jnp.logical_and(top, up_left == lon)
    self_right = jnp.logical_and(top, up_right == lon)
    down = jnp.where(bottom, lat, lat - 1)

    barrier = pltpu.get_barrier_semaphore()

    def greet(to_lon, to_lat):
        pl.semaphore_signal(
            barrier, inc=1, device_id={"lon": to_lon, "lat": to_lat}, device_id_type=MESH
        )

    @pl.when(jnp.logical_not(self_left))
    def _():
        greet(up_left, up)

    @pl.when(jnp.logical_not(self_right))
    def _():
        greet(up_right, up)

    @pl.when(jnp.logical_not(bottom))
    def _():
        greet(left, down)
        greet(right, down)
        greet(lon, down)

    greet(up_lon, up)
    greet(left, lat)
    greet(right, lat)

    arrays = (tracer, transport, diffusion, inverse_volume, sea_mask, regime)
    held = (in_tracer, in_transport, in_diffusion, in_volume, in_mask, in_regime)
    loads = [pltpu.make_async_copy(a, h, load_sem.at[i]) for i, (a, h) in enumerate(zip(arrays, held))]
    for load in loads:
        load.start()

    pad = jnp.zeros((8, LANES), F32)
    for ref in (field, guess, flux, planes):
        for i in range(ref.shape[0]):
            ref[i, pl.ds(0, 8)] = pad
            ref[i, pl.ds(8 + ROWS, 8)] = pad
    mask[pl.ds(ROWS + 8, 8)] = pad
    for ref in (lat_field, lat_guess, lat_flux):
        for i in range(ref.shape[0]):
            ref[i, pl.ds(0, 8)] = pad
            ref[i, pl.ds(56, 8)] = pad
    for ref in (lon_field, lon_guess, lon_flux):
        ref[0, pl.ds(0, 8)] = pad
        ref[0, pl.ds(24 + ROWS, 8)] = pad
    lat_mask[pl.ds(56, 8)] = pad
    lon_raw[4, pl.ds(ROWS + 16, 8)] = pad
    for i in range(2):
        edges[i, pl.ds(ROWS + 16, 8)] = pad

    @pl.when(bottom)
    def _():
        lat_edges[0] = jnp.zeros(lat_edges.shape[1:], F32)
        for i in range(2):
            edges[i, pl.ds(0, 8)] = pad

    for load in loads:
        load.wait()

    lane, row8 = iota(8, 1), iota(8, 0)
    place, west_side = lane & 7, lane < 64
    own_cell = jnp.where(west_side, place, LANES - 1 - place)
    own_east = jnp.where(
        west_side, place, jnp.where((lane & 15) >= 8, LANES - 2 - place, LANES - 1)
    )
    level_lane = (lane >> 4) & 1
    sent_cell = jnp.where(west_side, LANES - 8 + place, 7 - place)
    sent_east = jnp.where(west_side, LANES - 8 + place, jnp.maximum(6 - place, 0))
    swapped_cell = jnp.where(west_side, 7 - place, LANES - 8 + place)
    swapped_east = jnp.where(west_side, jnp.maximum(6 - place, 0), LANES - 8 + place)

    def reflected(n):
        return jnp.where(iota(n, 1) < 64, 1.0, -1.0)

    def own_strips(cells, moves, steady):
        n = cells[0].shape[0]
        channel, odd = (iota(n, 1) >> 4) & 3, ((iota(n, 1) >> 4) & 1) == 1
        got = [lanes_of(a, own_cell) for a in cells]
        cell = got[0]
        for ch in range(1, CHANNELS):
            cell = jnp.where(channel == ch, got[ch], cell)
        speed_east = [lanes_of(a, own_east) for a in moves[:2]]
        speed_north = [lanes_of(a, own_cell) for a in moves[2:]]
        return cell, [
            jnp.where(odd, speed_east[1], speed_east[0]) * reflected(n),
            jnp.where(odd, speed_north[1], speed_north[0]),
            lanes_of(steady[0], own_east),
            lanes_of(steady[1], own_cell),
            lanes_of(steady[2], own_cell),
            lanes_of(steady[3], own_east),
            lanes_of(steady[4], own_cell),
            lanes_of(steady[2], own_next),
        ]

    own_next = jnp.where(west_side, place + 1, LANES - 2 - place)

    def tile_rows(r, n):
        rows = pl.ds(r, n)
        sea = in_mask[rows].astype(F32)
        cells = [in_tracer[ch // 2, ch % 2, rows] * sea for ch in range(CHANNELS)]
        moves = [in_transport[j // 2, j % 2, rows] for j in range(4)]
        steady = [in_diffusion[j, rows] for j in range(2)]
        steady += [in_volume[rows] * sea]
        steady += [in_regime[j, rows].astype(F32) for j in range(2)]
        return sea, cells, moves, steady

    for i, r in ((0, 0), (1, ROWS - 8)):
        _, cells, moves, steady = tile_rows(r, 8)
        for k, tile in enumerate(cells + moves + steady):
            lat_packs[i, k] = tile

    def pack(i, carry):
        n = PACK
        r = pl.multiple_of(i * n, n)
        rows, padded = pl.ds(r, n), pl.ds(pl.multiple_of(r + 8, 8), n)
        sea, cells, moves, steady = tile_rows(r, n)
        mask[padded] = sea
        planes[12, padded] = steady[2]
        for ch in range(CHANNELS):
            field[ch, padded] = cells[ch]
        group, west_half = (iota(n, 1) >> 3) & 7, iota(n, 1) < 64
        first = lanes_of(cells[0], sent_cell)
        for ch in range(CHANNELS):
            if ch:
                first = jnp.where(group == 2 * ch, lanes_of(cells[ch], sent_cell), first)
            moved = lanes_of(moves[ch], sent_east if ch < 2 else sent_cell)
            first = jnp.where(group == 2 * ch + 1, moved * reflected(n) if ch < 2 else moved, first)
        second = lanes_of(steady[0], swapped_east)
        for k in range(1, 5):
            moved = lanes_of(steady[k], swapped_east if k == 3 else swapped_cell)
            second = jnp.where(group == k, moved, second)
        packs[0, rows] = jnp.where(west_half, second, first)
        packs[1, rows] = jnp.where(west_half, first, second)
        return carry

    lax.fori_loop(0, ROWS // PACK, pack, 0)

    def remote(src, dst, send, recv, to_lon, to_lat):
        return pltpu.make_async_remote_copy(
            src_ref=src,
            dst_ref=dst,
            send_sem=send,
            recv_sem=recv,
            device_id={"lon": to_lon, "lat": to_lat},
            device_id_type=MESH,
        )

    to_left = remote(packs.at[0], edges.at[1, pl.ds(8, ROWS)], lon_send.at[0], lon_recv.at[1], left, lat)
    to_right = remote(packs.at[1], edges.at[0, pl.ds(8, ROWS)], lon_send.at[1], lon_recv.at[0], right, lat)
    corner_row = pl.multiple_of(jnp.where(top, ROWS + 8, 0), 8)
    top_int = top.astype(jnp.int32)
    corner_ul = remote(
        packs.at[0, pl.ds(ROWS - 8, 8)],
        edges.at[1 - top_int, pl.ds(corner_row, 8)],
        corner_send.at[0],
        corner_recv.at[1 + top_int],
        up_left,
        up,
    )
    corner_ur = remote(
        packs.at[1, pl.ds(ROWS - 8, 8)],
        edges.at[top_int, pl.ds(corner_row, 8)],
        corner_send.at[1],
        corner_recv.at[3 * top_int],
        up_right,
        up,
    )
    corner_dl = remote(
        packs.at[0, pl.ds(0, 8)],
        edges.at[1, pl.ds(ROWS + 8, 8)],
        corner_send.at[2],
        corner_recv.at[3],
        left,
        down,
    )
    corner_dr = remote(
        packs.at[1, pl.ds(0, 8)],
        edges.at[0, pl.ds(ROWS + 8, 8)],
        corner_send.at[3],
        corner_recv.at[2],
        right,
        down,
    )
    to_up = remote(
        lat_packs.at[1], lat_edges.at[top_int], lat_send.at[0], lat_recv.at[top_int], up_lon, up
    )
    to_down = remote(lat_packs.at[0], lat_edges.at[1], lat_send.at[1], lat_recv.at[1], lon, down)

    pl.semaphore_wait(
        barrier,
        5
        - self_left.astype(jnp.int32)
        - self_right.astype(jnp.int32)
        + 3 * jnp.logical_not(bottom).astype(jnp.int32),
    )

    @pl.when(jnp.logical_not(self_left))
    def _():
        corner_ul.start()

    @pl.when(jnp.logical_not(self_right))
    def _():
        corner_ur.start()

    to_up.start()

    @pl.when(jnp.logical_not(bottom))
    def _():
        corner_dl.start()
        corner_dr.start()
        to_down.start()

    to_left.start()
    to_right.start()

    @pl.when(self_left)
    def _():
        edges[0, pl.ds(ROWS + 8, 8)] = packs[0, pl.ds(ROWS - 8, 8)]

    @pl.when(self_right)
    def _():
        edges[1, pl.ds(ROWS + 8, 8)] = packs[1, pl.ds(ROWS - 8, 8)]

    def prepare(i, carry):
        n = 64
        r = pl.multiple_of(i * n, n)
        rows, padded = pl.ds(r, n), pl.ds(pl.multiple_of(r + 8, 8), n)
        sea = mask[padded]
        open_east = sea * pltpu.roll(sea, LANES - 1, 1)
        open_north = sea * mask[pl.ds(r + 9, n)]
        regimes = [in_regime[j, rows].astype(F32) for j in range(2)]
        moves = [in_transport[j // 2, j % 2, rows] for j in range(4)]
        steady = [in_diffusion[j, rows] for j in range(2)] + [planes[12, padded]] + regimes
        for level in range(2):
            for way, opened in ((0, open_east), (1, open_north)):
                found = face_coefficients(moves[2 * way + level], steady[way], regimes[way], opened)
                for j in range(3):
                    planes[6 * level + 3 * way + j, padded] = found[j]
        cell, raw = own_strips([field[ch, padded] for ch in range(CHANNELS)], moves, steady)
        lon_field[0, pl.ds(pl.multiple_of(r + 16, 8), n)] = cell
        for a, strip in enumerate(raw):
            lon_raw[a, padded] = strip
        return carry

    lax.fori_loop(0, 4, prepare, 0)

    for ch in range(CHANNELS):
        lat_field[ch, pl.ds(16, 16)] = field[ch, pl.ds(8, 16)]
        lat_field[ch, pl.ds(32, 16)] = field[ch, pl.ds(ROWS - 8, 16)]
    for i in range(13):
        lat_planes[i, pl.ds(16, 16)] = planes[i, pl.ds(8, 16)]
        lat_planes[i, pl.ds(32, 16)] = planes[i, pl.ds(ROWS - 8, 16)]
    lat_mask[pl.ds(16, 16)] = mask[pl.ds(8, 16)]
    lat_mask[pl.ds(32, 16)] = mask[pl.ds(ROWS - 8, 16)]

    before = (lane - 2) & (LANES - 1)
    inner = 6 + ((lane + 2) & 3)
    patch_column = jnp.where(before < 64, inner, LANES - 1 - inner)

    def patch_lanes(n):
        return ((iota(n, 1) + 2) & 15) < 4

    def patch_of(channels):
        n = channels[0].shape[0]
        channel = (((iota(n, 1) - 2) & (LANES - 1)) >> 4) & 3
        got = [lanes_of(a, patch_column) for a in channels]
        result = got[0]
        for ch in range(1, CHANNELS):
            result = jnp.where(channel == ch, got[ch], result)
        return result

    def interior(step, carry):
        def run(source, target, kept, k):
            def chunk(i, c):
                start = pl.multiple_of(i * INNER + 8, 8)
                results = stage(source, target, kept, planes, flux, start, INNER, CHANNELS, 2)
                patches[k, pl.ds(start, INNER)] = patch_of(results)
                return c

            lax.fori_loop(0, ROWS // INNER, chunk, 0)

        run(field, guess, None, 2 * step)
        run(guess, field, field, 2 * step + 1)
        return carry

    lax.fori_loop(0, STEPS, interior, 0)

    remote(lat_edges.at[1], lat_edges.at[1], lat_send.at[0], lat_recv.at[1], lon, lat).wait_recv()

    @pl.when(jnp.logical_not(bottom))
    def _():
        remote(lat_edges.at[0], lat_edges.at[0], lat_send.at[0], lat_recv.at[0], lon, lat).wait_recv()

    row_cell, row_north = 7 - row8, jnp.maximum(6 - row8, 0)
    below = [lat_edges[0, k] for k in range(SENT)]
    norths = (6, 7, 9, 12)

    @pl.when(jnp.logical_not(top))
    def _():
        for k in range(SENT):
            lat_up[k] = lat_edges[1, k]

    @pl.when(top)
    def _():
        lane_cell, lane_east = LANES - 1 - lane, jnp.maximum(LANES - 2 - lane, 0)
        for k in range(SENT):
            turned = lanes(lat_edges[1, k], lane_east if k in (4, 5, 8, 11) else lane_cell)
            if k in (4, 5, 6, 7):
                turned = -turned
            lat_up[k] = sublanes(turned, row_north if k in norths else row_cell)
            if k in norths:
                lat_up[SENT + norths.index(k)] = sublanes(turned, row_cell)

    upper = [lat_up[k] for k in range(SENT)]
    lat_mask[pl.ds(8, 8)] = jnp.where(below[10] > 0.0, 1.0, 0.0)
    lat_mask[pl.ds(48, 8)] = jnp.where(upper[10] > 0.0, 1.0, 0.0)
    for ch in range(CHANNELS):
        lat_field[ch, pl.ds(8, 8)] = below[ch]
        lat_field[ch, pl.ds(48, 8)] = upper[ch]
    lat_planes[12, pl.ds(8, 8)] = below[10]
    lat_planes[12, pl.ds(48, 8)] = upper[10]
    highest = [lat_packs[1, k] for k in range(SENT)]
    for at, tiles in ((8, below), (40, highest), (48, upper)):
        sea = lat_mask[pl.ds(at, 8)]
        opened = (sea * pltpu.roll(sea, LANES - 1, 1), sea * lat_mask[pl.ds(at + 1, 8)])
        for level in range(2):
            for way in range(2):
                found = face_coefficients(
                    tiles[4 + 2 * way + level], tiles[8 + way], tiles[11 + way], opened[way]
                )
                for j in range(3):
                    lat_planes[6 * level + 3 * way + j, pl.ds(at, 8)] = found[j]

    @pl.when(jnp.logical_not(top))
    def _():
        for level in range(2):
            for j in range(3):
                lat_second[3 * level + j] = lat_planes[6 * level + 3 + j, pl.ds(47, 8)]

    @pl.when(top)
    def _():
        opened = lat_mask[pl.ds(47, 8)] * lat_mask[pl.ds(48, 8)]
        for level in range(2):
            found = face_coefficients(lat_up[13 + level], lat_up[15], lat_up[16], opened)
            for j in range(3):
                lat_second[3 * level + j] = found[j]

    lat_pair, lon_pair = (lat_field, lat_guess), (lon_field, lon_guess)
    for k in range(2 * STEPS):
        results = stage(
            lat_pair[k % 2],
            lat_pair[(k + 1) % 2],
            lat_field if k % 2 else None,
            lat_planes,
            lat_flux,
            8,
            48,
            CHANNELS,
            2,
            fold=(lat_second, 48),
        )
        if k < 2 * STEPS - 1:
            for at, to in ((0, 0), (32, ROWS)):
                patches[k, pl.ds(to, 16)] = patch_of([r[at : at + 16] for r in results])
    for ch in range(CHANNELS):
        field[ch, pl.ds(8, 8)] = lat_field[ch, pl.ds(16, 8)]
        field[ch, pl.ds(ROWS, 8)] = lat_field[ch, pl.ds(40, 8)]

    @pl.when(jnp.logical_not(bottom))
    def _():
        for side in range(2):
            remote(
                edges.at[side, pl.ds(0, 8)],
                edges.at[side, pl.ds(0, 8)],
                corner_send.at[0],
                corner_recv.at[side],
                lon,
                lat,
            ).wait_recv()

    @pl.when(jnp.logical_not(self_left))
    def _():
        remote(
            edges.at[0, pl.ds(ROWS + 8, 8)],
            edges.at[0, pl.ds(ROWS + 8, 8)],
            corner_send.at[0],
            corner_recv.at[2],
            lon,
            lat,
        ).wait_recv()

    @pl.when(jnp.logical_not(self_right))
    def _():
        remote(
            edges.at[1, pl.ds(ROWS + 8, 8)],
            edges.at[1, pl.ds(ROWS + 8, 8)],
            corner_send.at[0],
            corner_recv.at[3],
            lon,
            lat,
        ).wait_recv()

    for side in range(2):
        remote(
            edges.at[side, pl.ds(8, ROWS)],
            edges.at[side, pl.ds(8, ROWS)],
            lon_send.at[0],
            lon_recv.at[side],
            lon,
            lat,
        ).wait_recv()

    half = lane & 64
    far_index = [half + 16 * (j + level_lane) + 8 + place for j in (0, 2)]
    far_index += [(64 - half) + 8 * j + place for j in range(5)]

    def far_strips(west_edge, east_edge):
        west_half = iota(west_edge.shape[0], 1) < 64
        first = jnp.where(west_half, west_edge, east_edge)
        second = jnp.where(west_half, east_edge, west_edge)
        return first, [lanes_of(first if a < 2 else second, far_index[a]) for a in range(7)]

    def own_lanes(n, a):
        spot = iota(n, 1)
        if a in (0, 2, 5):
            return (spot & 15) >= jnp.where(spot < 64, 8, 7)
        return (spot & 15) >= 8

    cell, raw = own_strips(below[:4], below[4:8], below[8:])
    lon_field[0, pl.ds(8, 8)] = cell
    for a, strip in enumerate(raw):
        lon_raw[a, pl.ds(0, 8)] = strip

    @pl.when(jnp.logical_not(top))
    def _():
        cell, raw = own_strips(upper[:4], upper[4:8], upper[8:])
        lon_field[0, pl.ds(ROWS + 16, 8)] = cell
        for a, strip in enumerate(raw):
            lon_raw[a, pl.ds(ROWS + 8, 8)] = strip

    @pl.when(top)
    def _():
        across = [lat_edges[1, k] for k in range(SENT)]
        cell, raw = own_strips(across[:4], across[4:8], across[8:])
        far_cell, far_raw = far_strips(edges[1, pl.ds(ROWS + 8, 8)], edges[0, pl.ds(ROWS + 8, 8)])
        cell = jnp.where(own_lanes(8, 1), cell, far_cell)
        lon_field[0, pl.ds(ROWS + 16, 8)] = sublanes(pltpu.roll(cell, 64, 1), row_cell)
        for a in range(8):
            strip = raw[a] if a == 7 else jnp.where(own_lanes(8, a), raw[a], far_raw[a])
            turned = pltpu.roll(strip, 64, 1)
            if a == 1:
                turned = -turned
            lon_raw[a, pl.ds(ROWS + 8, 8)] = sublanes(turned, row_north if a in (1, 3, 6) else row_cell)
            if a in (1, 3, 6):
                lon_second[(1, 3, 6).index(a)] = sublanes(turned, row_cell)

    def join(i, carry):
        n = JOIN
        r = pl.multiple_of(i * n, 8)
        rows, padded = pl.ds(r, n), pl.ds(pl.multiple_of(r + 8, 8), n)
        whole = jnp.logical_and(iota(n, 0) + r >= ROWS + 8, top)
        whole_next = jnp.logical_and(iota(n, 0) + r >= ROWS + 7, top)
        west_edge, east_edge = edges[0, rows], edges[1, rows]
        first, far = far_strips(west_edge, east_edge)
        lon_field[0, padded] = jnp.where(
            jnp.logical_or(own_lanes(n, 1), whole), lon_field[0, padded], first
        )
        speed_east, speed_north, east_mix, north_mix, volume, east_rule, north_rule = [
            jnp.where(jnp.logical_or(own_lanes(n, a), whole), lon_raw[a, rows], far[a]) for a in range(7)
        ]
        lon_planes[6, padded] = volume
        ahead = pl.ds(r + 1, n)
        next_row = jnp.where(iota(n, 1) < 64, edges[1, ahead], edges[0, ahead])
        next_volume = jnp.where(
            jnp.logical_or(own_lanes(n, 4), whole_next),
            lon_raw[4, ahead],
            lanes_of(next_row, far_index[4]),
        )
        sea = jnp.where(volume > 0.0, 1.0, 0.0)
        sea_north = jnp.where(next_volume > 0.0, 1.0, 0.0)
        beyond_slot = jnp.where(lon_raw[7, rows] > 0.0, 1.0, 0.0)
        sea_east = jnp.where((iota(n, 1) & 15) == 15, beyond_slot, pltpu.roll(sea, LANES - 1, 1))
        found = face_coefficients(speed_east, east_mix, east_rule, sea * sea_east)
        found += face_coefficients(speed_north, north_mix, north_rule, sea * sea_north)
        for j in range(6):
            lon_planes[j, padded] = found[j]
        return carry

    lax.fori_loop(0, (ROWS + 16) // JOIN, join, 0)

    @pl.when(jnp.logical_not(top))
    def _():
        for j in range(3):
            lon_second[j] = lon_planes[3 + j, pl.ds(ROWS + 15, 8)]

    @pl.when(top)
    def _():
        seas = [jnp.where(lon_planes[6, pl.ds(ROWS + 15 + i, 8)] > 0.0, 1.0, 0.0) for i in range(2)]
        found = face_coefficients(*[lon_second[j] for j in range(3)], seas[0] * seas[1])
        for j in range(3):
            lon_second[j] = found[j]

    for k in range(2 * STEPS):
        last = k == 2 * STEPS - 1

        def patch(result):
            return jnp.where(patch_lanes(ROWS + 16), patches[k, pl.ds(0, ROWS + 16)], result)

        stage(
            lon_pair[k % 2],
            lon_pair[(k + 1) % 2],
            lon_field if k % 2 else None,
            lon_planes,
            lon_flux,
            8,
            ROWS + 16,
            1,
            1,
            fold=(lon_second, ROWS + 16),
            patch=None if last else patch,
        )

    def finish(i, carry):
        n = 128
        r = pl.multiple_of(i * n, n)
        rows, padded = pl.ds(r, n), pl.ds(pl.multiple_of(r + 8, 8), n)
        edge = lon_field[0, pl.ds(pl.multiple_of(r + 16, 8), n)]
        wide = iota(n, 1)
        kept = jnp.logical_and(wide >= 8, wide < LANES - 8)
        for ch in range(CHANNELS):
            index = 16 * ch + 8 + jnp.where(west_side, place, 64 + 7 - place)
            out[ch // 2, ch % 2, rows] = jnp.where(kept, field[ch, padded], lanes_of(edge, index))
        return carry

    lax.fori_loop(0, 2, finish, 0)

    to_left.wait_send()
    to_right.wait_send()
    to_up.wait_send()

    @pl.when(jnp.logical_not(self_left))
    def _():
        corner_ul.wait_send()

    @pl.when(jnp.logical_not(self_right))
    def _():
        corner_ur.wait_send()

    @pl.when(jnp.logical_not(bottom))
    def _():
        corner_dl.wait_send()
        corner_dr.wait_send()
        to_down.wait_send()


def solution(mesh):
    lon_count, lat_count = mesh.shape["lon"], mesh.shape["lat"]
    placed = (
        P(None, None, "lat", "lon"),
        P(None, None, "lat", "lon"),
        P(None, "lat", "lon"),
        P("lat", "lon"),
        P("lat", "lon"),
        P(None, "lat", "lon"),
    )

    def local(*arrays):
        shapes = [a.shape for a in arrays]
        types = [a.dtype for a in arrays]
        tall, wide = ROWS + 16, ROWS + 32

        def vmem(*shape):
            return pltpu.VMEM(shape, F32)

        return pl.pallas_call(
            functools.partial(kernel, lon_count, lat_count),
            out_shape=pltpu.VMEM(shapes[0], F32),
            in_specs=[pl.BlockSpec(memory_space=pl.ANY)] * 6,
            out_specs=pl.BlockSpec(memory_space=pltpu.VMEM),
            scratch_shapes=[
                *[pltpu.VMEM(s, t) for s, t in zip(shapes, types)],
                vmem(tall, LANES),
                vmem(CHANNELS, tall, LANES),
                vmem(CHANNELS, tall, LANES),
                vmem(13, tall, LANES),
                vmem(CHANNELS, tall, LANES),
                vmem(2, ROWS, LANES),
                vmem(2, tall + 8, LANES),
                vmem(2, SENT, 8, LANES),
                vmem(2, SENT, 8, LANES),
                vmem(64, LANES),
                vmem(CHANNELS, 64, LANES),
                vmem(CHANNELS, 64, LANES),
                vmem(13, 64, LANES),
                vmem(CHANNELS, 64, LANES),
                vmem(SENT + 4, 8, LANES),
                vmem(6, 8, LANES),
                vmem(8, tall + 8, LANES),
                vmem(1, wide, LANES),
                vmem(1, wide, LANES),
                vmem(7, wide, LANES),
                vmem(1, wide, LANES),
                vmem(3, 8, LANES),
                vmem(2 * STEPS, tall, LANES),
                pltpu.SemaphoreType.DMA((6,)),
                pltpu.SemaphoreType.DMA((2,)),
                pltpu.SemaphoreType.DMA((2,)),
                pltpu.SemaphoreType.DMA((2,)),
                pltpu.SemaphoreType.DMA((2,)),
                pltpu.SemaphoreType.DMA((4,)),
                pltpu.SemaphoreType.DMA((4,)),
            ],
            compiler_params=pltpu.CompilerParams(
                collective_id=0, has_side_effects=True, vmem_limit_bytes=64900 * 1024
            ),
        )(*arrays)

    return jax.shard_map(
        local, mesh=mesh, in_specs=placed, out_specs=P(None, None, "lat", "lon"), check_vma=False
    )
```

time: 30 us -> 17.4 us (0.58)
  the two profiles are of different devices: /device:TPU:4 before, /device:TPU:29 now
where the time goes in v2:
time: 17.4 us; the launch traced here: 17.3 us
  Pallas kernels  16.5 us (95%)
  local copies, waits for them, and re-layouts  0.8 us (5%)
    pallas_call x1, Pallas kernels, local(): pl.pallas_call(functools.partial(kernel, lon_count, lat_count), out_shape...  16.5 us
    unnamed x1, local copies, waits for them, and re-layouts  0.8 us

profile of v2, /device:TPU:29, one launch (start us, length us, event | category | flops | bytes accessed | tf_op | source)
XLA Modules:
  0.0 17.3 jit_solution(6406984369972612198)
XLA Ops:
  0.0 16.5 %shard_map.64 = f32[2,2,256,128]{3,2,1,0:T(8,128)S(1)} custom-call(f32[2,2,256,128]{3,2,1,0:T(8,128)} %tracer.1, f32[2,2,256,128]{3,2,1,0:T(8,128)} %transport.1, f32[2,256,128]{2,1,0:T(8,128)} %diffusion.1, f32[256,128]{1,0:T(8,128)} %inverse_volume.1, s32[256,128]{1,0:T(8,128)} %sea_mask.1, s32[2,256,128]{2,1,0:T(8,128)} %regime.1), custom_call_target="tpu_custom_call" | custom-call | tf_op jit(solution)/shard_map/pallas_call | solution.py:744
  16.5 0.8 %copy.8 = f32[2,2,256,128]{3,2,1,0:T(8,128)} copy(f32[2,2,256,128]{3,2,1,0:T(8,128)S(1)} %shard_map.64) | data formatting | bytes 1048576

commit v3 on v2

--- a/solution.py
+++ b/solution.py
@@ -15,8 +15,9 @@
 CHANNELS = 4
 F32 = jnp.float32
 INNER = 256
-PACK = 64
+PREP = 64
 JOIN = 136
+GROUP = 72
 
 SENT = 13
 
@@ -107,6 +108,56 @@
     return results
 
 
+def unit(source, target, kept, planes, north_flux, ch, levels, start, count, fold, patch, results):
+    rows, level = pl.ds(start, count), 6 * (ch % levels)
+    cell = source[ch, rows]
+    east1 = pltpu.roll(cell, LANES - 1, 1)
+    west1 = pltpu.roll(cell, 1, 1)
+    east2 = pltpu.roll(cell, LANES - 2, 1)
+    yield
+    behind = source[ch, pl.ds(start - 1, count)]
+    ahead = source[ch, pl.ds(start + 1, count)]
+    beyond = source[ch, pl.ds(start + 2, count)]
+    north = face_flux(
+        cell, ahead - cell, cell - behind, beyond - ahead, *[planes[level + i, rows] for i in (3, 4, 5)]
+    )
+    north_flux[ch, rows] = north
+    if fold is not None and start <= fold[1] - 1 < start + count:
+        second, row = fold
+        at = [source[ch, pl.ds(row + i, 8)] for i in (-2, -1, 0, 1)]
+        theirs = face_flux(
+            at[1],
+            at[2] - at[1],
+            at[1] - at[0],
+            at[3] - at[2],
+            *[second[3 * (ch % levels) + i] for i in range(3)],
+        )
+        north_flux[ch, pl.ds(row - 1, 1)] = theirs[0:1]
+    yield
+    east = face_flux(
+        cell, east1 - cell, cell - west1, east2 - east1, *[planes[level + i, rows] for i in range(3)]
+    )
+    west = pltpu.roll(east, 1, 1)
+    yield
+    south = north_flux[ch, pl.ds(start - 1, count)]
+    result = planes[6 * levels, rows] * ((west - east) + (south - north))
+    if kept is None:
+        result = cell + result
+    else:
+        result = 0.5 * ((kept[ch, rows] + cell) + result)
+    if patch is not None:
+        result = patch(result, rows)
+    target[ch, rows] = result
+    results.append(result)
+
+
+def pipeline(units):
+    for turn in range(len(units) + 3):
+        for phase in range(4):
+            if 0 <= turn - phase < len(units):
+                next(units[turn - phase], None)
+
+
 def kernel(
     lon_count,
     lat_count,
@@ -137,7 +188,6 @@
     lat_guess,
     lat_planes,
     lat_flux,
-    lat_up,
     lat_second,
     lon_raw,
     lon_field,
@@ -278,10 +328,8 @@
         for k, tile in enumerate(cells + moves + steady):
             lat_packs[i, k] = tile
 
-    def pack(i, carry):
-        n = PACK
-        r = pl.multiple_of(i * n, n)
-        rows, padded = pl.ds(r, n), pl.ds(pl.multiple_of(r + 8, 8), n)
+    def pack(r, n):
+        rows, padded = pl.ds(r, n), pl.ds(r + 8, n)
         sea, cells, moves, steady = tile_rows(r, n)
         mask[padded] = sea
         planes[12, padded] = steady[2]
@@ -300,9 +348,8 @@
             second = jnp.where(group == k, moved, second)
         packs[0, rows] = jnp.where(west_half, second, first)
         packs[1, rows] = jnp.where(west_half, first, second)
-        return carry
-
-    lax.fori_loop(0, ROWS // PACK, pack, 0)
+
+    pack(0, ROWS)
 
     def remote(src, dst, send, recv, to_lon, to_lat):
         return pltpu.make_async_remote_copy(
@@ -390,10 +437,8 @@
     def _():
         edges[1, pl.ds(ROWS + 8, 8)] = packs[1, pl.ds(ROWS - 8, 8)]
 
-    def prepare(i, carry):
-        n = 64
-        r = pl.multiple_of(i * n, n)
-        rows, padded = pl.ds(r, n), pl.ds(pl.multiple_of(r + 8, 8), n)
+    def prepare(r, n):
+        rows, padded = pl.ds(r, n), pl.ds(r + 8, n)
         sea = mask[padded]
         open_east = sea * pltpu.roll(sea, LANES - 1, 1)
         open_north = sea * mask[pl.ds(r + 9, n)]
@@ -406,12 +451,12 @@
                 for j in range(3):
                     planes[6 * level + 3 * way + j, padded] = found[j]
         cell, raw = own_strips([field[ch, padded] for ch in range(CHANNELS)], moves, steady)
-        lon_field[0, pl.ds(pl.multiple_of(r + 16, 8), n)] = cell
+        lon_field[0, pl.ds(r + 16, n)] = cell
         for a, strip in enumerate(raw):
             lon_raw[a, padded] = strip
-        return carry
-
-    lax.fori_loop(0, 4, prepare, 0)
+
+    for r in range(0, ROWS, PREP):
+        prepare(r, PREP)
 
     for ch in range(CHANNELS):
         lat_field[ch, pl.ds(16, 16)] = field[ch, pl.ds(8, 16)]
@@ -460,27 +505,23 @@
     def _():
         remote(lat_edges.at[0], lat_edges.at[0], lat_send.at[0], lat_recv.at[0], lon, lat).wait_recv()
 
-    row_cell, row_north = 7 - row8, jnp.maximum(6 - row8, 0)
     below = [lat_edges[0, k] for k in range(SENT)]
+    across = [lat_edges[1, k] for k in range(SENT)]
     norths = (6, 7, 9, 12)
-
-    @pl.when(jnp.logical_not(top))
-    def _():
-        for k in range(SENT):
-            lat_up[k] = lat_edges[1, k]
-
-    @pl.when(top)
-    def _():
-        lane_cell, lane_east = LANES - 1 - lane, jnp.maximum(LANES - 2 - lane, 0)
-        for k in range(SENT):
-            turned = lanes(lat_edges[1, k], lane_east if k in (4, 5, 8, 11) else lane_cell)
-            if k in (4, 5, 6, 7):
-                turned = -turned
-            lat_up[k] = sublanes(turned, row_north if k in norths else row_cell)
-            if k in norths:
-                lat_up[SENT + norths.index(k)] = sublanes(turned, row_cell)
-
-    upper = [lat_up[k] for k in range(SENT)]
+    row_cell = jnp.where(top, 7 - row8, row8)
+    row_north = jnp.where(top, jnp.maximum(6 - row8, 0), row8)
+    sign = jnp.where(top, -1.0, 1.0)
+    lane_cell = jnp.where(top, LANES - 1 - lane, lane)
+    lane_east = jnp.where(top, jnp.maximum(LANES - 2 - lane, 0), lane)
+    upper, second_raw = [], []
+    for k in range(SENT):
+        turned = lanes(across[k], lane_east if k in (4, 5, 8, 11) else lane_cell)
+        if k in (4, 5, 6, 7):
+            turned = turned * sign
+        upper.append(sublanes(turned, row_north if k in norths else row_cell))
+        if k in norths:
+            second_raw.append(sublanes(turned, row_cell))
+
     lat_mask[pl.ds(8, 8)] = jnp.where(below[10] > 0.0, 1.0, 0.0)
     lat_mask[pl.ds(48, 8)] = jnp.where(upper[10] > 0.0, 1.0, 0.0)
     for ch in range(CHANNELS):
@@ -500,40 +541,70 @@
                 for j in range(3):
                     lat_planes[6 * level + 3 * way + j, pl.ds(at, 8)] = found[j]
 
-    @pl.when(jnp.logical_not(top))
-    def _():
-        for level in range(2):
-            for j in range(3):
-                lat_second[3 * level + j] = lat_planes[6 * level + 3 + j, pl.ds(47, 8)]
-
-    @pl.when(top)
-    def _():
-        opened = lat_mask[pl.ds(47, 8)] * lat_mask[pl.ds(48, 8)]
-        for level in range(2):
-            found = face_coefficients(lat_up[13 + level], lat_up[15], lat_up[16], opened)
-            for j in range(3):
-                lat_second[3 * level + j] = found[j]
+    opened = lat_mask[pl.ds(47, 8)] * lat_mask[pl.ds(48, 8)]
+    for level in range(2):
+        found = face_coefficients(second_raw[level], second_raw[2], second_raw[3], opened)
+        for j in range(3):
+            lat_second[3 * level + j] = jnp.where(top, found[j], lat_planes[6 * level + 3 + j, pl.ds(47, 8)])
 
     lat_pair, lon_pair = (lat_field, lat_guess), (lon_field, lon_guess)
-    for k in range(2 * STEPS):
-        results = stage(
-            lat_pair[k % 2],
-            lat_pair[(k + 1) % 2],
-            lat_field if k % 2 else None,
-            lat_planes,
-            lat_flux,
-            8,
-            48,
-            CHANNELS,
-            2,
-            fold=(lat_second, 48),
-        )
+
+    def lat_units(k, results):
+        return [
+            unit(
+                lat_pair[k % 2],
+                lat_pair[(k + 1) % 2],
+                lat_field if k % 2 else None,
+                lat_planes,
+                lat_flux,
+                ch,
+                2,
+                start,
+                count,
+                (lat_second, 48),
+                None,
+                results,
+            )
+            for ch in range(CHANNELS)
+            for start, count in (((8, 48),) if k < 2 * STEPS - 1 else ((8, 16), (32, 16)))
+        ]
+
+    def lon_units(k):
+        def patch(result, rows):
+            n = result.shape[0]
+            return jnp.where(patch_lanes(n), patches[k, pl.ds(rows.start - 8, n)], result)
+
+        return [
+            unit(
+                lon_pair[k % 2],
+                lon_pair[(k + 1) % 2],
+                lon_field if k % 2 else None,
+                lon_planes,
+                lon_flux,
+                0,
+                1,
+                8 + r,
+                min(GROUP, ROWS + 16 - r),
+                (lon_second, ROWS + 16),
+                None if k == 2 * STEPS - 1 else patch,
+                [],
+            )
+            for r in range(0, ROWS + 16, GROUP)
+        ]
+
+    def lat_done(k, results):
         if k < 2 * STEPS - 1:
             for at, to in ((0, 0), (32, ROWS)):
                 patches[k, pl.ds(to, 16)] = patch_of([r[at : at + 16] for r in results])
-    for ch in range(CHANNELS):
-        field[ch, pl.ds(8, 8)] = lat_field[ch, pl.ds(16, 8)]
-        field[ch, pl.ds(ROWS, 8)] = lat_field[ch, pl.ds(40, 8)]
+        else:
+            for ch in range(CHANNELS):
+                field[ch, pl.ds(8, 8)] = lat_field[ch, pl.ds(16, 8)]
+                field[ch, pl.ds(ROWS, 8)] = lat_field[ch, pl.ds(40, 8)]
+
+    for k in range(2 * STEPS):
+        results = []
+        pipeline(lat_units(k, results))
+        lat_done(k, results)
 
     @pl.when(jnp.logical_not(bottom))
     def _():
@@ -600,35 +671,28 @@
     for a, strip in enumerate(raw):
         lon_raw[a, pl.ds(0, 8)] = strip
 
-    @pl.when(jnp.logical_not(top))
-    def _():
-        cell, raw = own_strips(upper[:4], upper[4:8], upper[8:])
-        lon_field[0, pl.ds(ROWS + 16, 8)] = cell
-        for a, strip in enumerate(raw):
-            lon_raw[a, pl.ds(ROWS + 8, 8)] = strip
-
-    @pl.when(top)
-    def _():
-        across = [lat_edges[1, k] for k in range(SENT)]
-        cell, raw = own_strips(across[:4], across[4:8], across[8:])
-        far_cell, far_raw = far_strips(edges[1, pl.ds(ROWS + 8, 8)], edges[0, pl.ds(ROWS + 8, 8)])
-        cell = jnp.where(own_lanes(8, 1), cell, far_cell)
-        lon_field[0, pl.ds(ROWS + 16, 8)] = sublanes(pltpu.roll(cell, 64, 1), row_cell)
-        for a in range(8):
-            strip = raw[a] if a == 7 else jnp.where(own_lanes(8, a), raw[a], far_raw[a])
-            turned = pltpu.roll(strip, 64, 1)
-            if a == 1:
-                turned = -turned
-            lon_raw[a, pl.ds(ROWS + 8, 8)] = sublanes(turned, row_north if a in (1, 3, 6) else row_cell)
-            if a in (1, 3, 6):
-                lon_second[(1, 3, 6).index(a)] = sublanes(turned, row_cell)
-
-    def join(i, carry):
-        n = JOIN
-        r = pl.multiple_of(i * n, 8)
-        rows, padded = pl.ds(r, n), pl.ds(pl.multiple_of(r + 8, 8), n)
-        whole = jnp.logical_and(iota(n, 0) + r >= ROWS + 8, top)
-        whole_next = jnp.logical_and(iota(n, 0) + r >= ROWS + 7, top)
+    cell, raw = own_strips(across[:4], across[4:8], across[8:])
+    corners = [edges[side, pl.ds(ROWS + 8, 8)] for side in range(2)]
+    far_cell, far_raw = far_strips(
+        jnp.where(top, corners[1], corners[0]), jnp.where(top, corners[0], corners[1])
+    )
+    side_swap = jnp.where(top, lane ^ 64, lane)
+    cell = lanes(jnp.where(own_lanes(8, 1), cell, far_cell), side_swap)
+    lon_field[0, pl.ds(ROWS + 16, 8)] = sublanes(cell, row_cell)
+    second_raw = []
+    for a in range(8):
+        strip = raw[a] if a == 7 else jnp.where(own_lanes(8, a), raw[a], far_raw[a])
+        turned = lanes(strip, side_swap)
+        if a == 1:
+            turned = turned * sign
+        lon_raw[a, pl.ds(ROWS + 8, 8)] = sublanes(turned, row_north if a in (1, 3, 6) else row_cell)
+        if a in (1, 3, 6):
+            second_raw.append(sublanes(turned, row_cell))
+
+    def join(r, n):
+        rows, padded = pl.ds(r, n), pl.ds(r + 8, n)
+        whole = iota(n, 0) + r >= ROWS + 8
+        whole_next = iota(n, 0) + r >= ROWS + 7
         west_edge, east_edge = edges[0, rows], edges[1, rows]
         first, far = far_strips(west_edge, east_edge)
         lon_field[0, padded] = jnp.where(
@@ -653,55 +717,28 @@
         found += face_coefficients(speed_north, north_mix, north_rule, sea * sea_north)
         for j in range(6):
             lon_planes[j, padded] = found[j]
-        return carry
-
-    lax.fori_loop(0, (ROWS + 16) // JOIN, join, 0)
-
-    @pl.when(jnp.logical_not(top))
-    def _():
-        for j in range(3):
-            lon_second[j] = lon_planes[3 + j, pl.ds(ROWS + 15, 8)]
-
-    @pl.when(top)
-    def _():
-        seas = [jnp.where(lon_planes[6, pl.ds(ROWS + 15 + i, 8)] > 0.0, 1.0, 0.0) for i in range(2)]
-        found = face_coefficients(*[lon_second[j] for j in range(3)], seas[0] * seas[1])
-        for j in range(3):
-            lon_second[j] = found[j]
+
+    for r in range(0, ROWS + 16, JOIN):
+        join(r, JOIN)
+
+    seas = [jnp.where(lon_planes[6, pl.ds(ROWS + 15 + i, 8)] > 0.0, 1.0, 0.0) for i in range(2)]
+    found = face_coefficients(*second_raw, seas[0] * seas[1])
+    for j in range(3):
+        lon_second[j] = jnp.where(top, found[j], lon_planes[3 + j, pl.ds(ROWS + 15, 8)])
 
     for k in range(2 * STEPS):
-        last = k == 2 * STEPS - 1
-
-        def patch(result):
-            return jnp.where(patch_lanes(ROWS + 16), patches[k, pl.ds(0, ROWS + 16)], result)
-
-        stage(
-            lon_pair[k % 2],
-            lon_pair[(k + 1) % 2],
-            lon_field if k % 2 else None,
-            lon_planes,
-            lon_flux,
-            8,
-            ROWS + 16,
-            1,
-            1,
-            fold=(lon_second, ROWS + 16),
-            patch=None if last else patch,
-        )
-
-    def finish(i, carry):
-        n = 128
-        r = pl.multiple_of(i * n, n)
-        rows, padded = pl.ds(r, n), pl.ds(pl.multiple_of(r + 8, 8), n)
-        edge = lon_field[0, pl.ds(pl.multiple_of(r + 16, 8), n)]
+        pipeline(lon_units(k))
+
+    def finish(r, n):
+        rows, padded = pl.ds(r, n), pl.ds(r + 8, n)
+        edge = lon_field[0, pl.ds(r + 16, n)]
         wide = iota(n, 1)
         kept = jnp.logical_and(wide >= 8, wide < LANES - 8)
         for ch in range(CHANNELS):
             index = 16 * ch + 8 + jnp.where(west_side, place, 64 + 7 - place)
             out[ch // 2, ch % 2, rows] = jnp.where(kept, field[ch, padded], lanes_of(edge, index))
-        return carry
-
-    lax.fori_loop(0, 2, finish, 0)
+
+    finish(0, ROWS)
 
     to_left.wait_send()
     to_right.wait_send()
@@ -762,7 +799,6 @@
                 vmem(CHANNELS, 64, LANES),
                 vmem(13, 64, LANES),
                 vmem(CHANNELS, 64, LANES),
-                vmem(SENT + 4, 8, LANES),
                 vmem(6, 8, LANES),
                 vmem(8, tall + 8, LANES),
                 vmem(1, wide, LANES),

time: 17.4 us -> 16.4 us (0.943)
  the two profiles are of different devices: /device:TPU:29 before, /device:TPU:4 now
where the time goes in v3:
time: 16.4 us; the launch traced here: 16.1 us
  Pallas kernels  15.3 us (93%)
  local copies, waits for them, and re-layouts  0.8 us (5%)
    pallas_call x1, Pallas kernels, local(): pl.pallas_call(functools.partial(kernel, lon_count, lat_count), out_shape...  15.3 us
    unnamed x1, local copies, waits for them, and re-layouts  0.8 us

profile of v3, /device:TPU:4, one launch (start us, length us, event | category | flops | bytes accessed | tf_op | source)
XLA Modules:
  0.0 16.1 jit_solution(17529627936097514267)
XLA Ops:
  0.0 15.3 %shard_map.64 = f32[2,2,256,128]{3,2,1,0:T(8,128)S(1)} custom-call(f32[2,2,256,128]{3,2,1,0:T(8,128)} %tracer.1, f32[2,2,256,128]{3,2,1,0:T(8,128)} %transport.1, f32[2,256,128]{2,1,0:T(8,128)} %diffusion.1, f32[256,128]{1,0:T(8,128)} %inverse_volume.1, s32[256,128]{1,0:T(8,128)} %sea_mask.1, s32[2,256,128]{2,1,0:T(8,128)} %regime.1), custom_call_target="tpu_custom_call" | custom-call | tf_op jit(solution)/shard_map/pallas_call | solution.py:781
  15.3 0.8 %copy.8 = f32[2,2,256,128]{3,2,1,0:T(8,128)} copy(f32[2,2,256,128]{3,2,1,0:T(8,128)S(1)} %shard_map.64) | data formatting | bytes 1048576

commit v4 on v3

--- a/solution.py
+++ b/solution.py
@@ -16,7 +16,6 @@
 F32 = jnp.float32
 INNER = 256
 PREP = 64
-JOIN = 136
 GROUP = 72
 
 SENT = 13
@@ -402,32 +401,39 @@
     )
     to_down = remote(lat_packs.at[0], lat_edges.at[1], lat_send.at[1], lat_recv.at[1], lon, down)
 
-    pl.semaphore_wait(
-        barrier,
-        5
-        - self_left.astype(jnp.int32)
-        - self_right.astype(jnp.int32)
-        + 3 * jnp.logical_not(bottom).astype(jnp.int32),
-    )
-
-    @pl.when(jnp.logical_not(self_left))
-    def _():
-        corner_ul.start()
-
-    @pl.when(jnp.logical_not(self_right))
-    def _():
-        corner_ur.start()
-
-    to_up.start()
-
-    @pl.when(jnp.logical_not(bottom))
-    def _():
-        corner_dl.start()
-        corner_dr.start()
-        to_down.start()
-
-    to_left.start()
-    to_right.start()
+    def dispatch():
+        pl.semaphore_wait(
+            barrier,
+            5
+            - self_left.astype(jnp.int32)
+            - self_right.astype(jnp.int32)
+            + 3 * jnp.logical_not(bottom).astype(jnp.int32),
+        )
+
+        @pl.when(jnp.logical_not(self_left))
+        def _():
+            corner_ul.start()
+
+        @pl.when(jnp.logical_not(self_right))
+        def _():
+            corner_ur.start()
+
+        to_up.start()
+
+        @pl.when(jnp.logical_not(bottom))
+        def _():
+            corner_dl.start()
+            corner_dr.start()
+            to_down.start()
+
+        to_left.start()
+        to_right.start()
+
+    early = lon == 0
+
+    @pl.when(jnp.logical_not(early))
+    def _():
+        dispatch()
 
     @pl.when(self_left)
     def _():
@@ -499,156 +505,9 @@
 
     lax.fori_loop(0, STEPS, interior, 0)
 
-    remote(lat_edges.at[1], lat_edges.at[1], lat_send.at[0], lat_recv.at[1], lon, lat).wait_recv()
-
-    @pl.when(jnp.logical_not(bottom))
-    def _():
-        remote(lat_edges.at[0], lat_edges.at[0], lat_send.at[0], lat_recv.at[0], lon, lat).wait_recv()
-
-    below = [lat_edges[0, k] for k in range(SENT)]
-    across = [lat_edges[1, k] for k in range(SENT)]
-    norths = (6, 7, 9, 12)
-    row_cell = jnp.where(top, 7 - row8, row8)
-    row_north = jnp.where(top, jnp.maximum(6 - row8, 0), row8)
-    sign = jnp.where(top, -1.0, 1.0)
-    lane_cell = jnp.where(top, LANES - 1 - lane, lane)
-    lane_east = jnp.where(top, jnp.maximum(LANES - 2 - lane, 0), lane)
-    upper, second_raw = [], []
-    for k in range(SENT):
-        turned = lanes(across[k], lane_east if k in (4, 5, 8, 11) else lane_cell)
-        if k in (4, 5, 6, 7):
-            turned = turned * sign
-        upper.append(sublanes(turned, row_north if k in norths else row_cell))
-        if k in norths:
-            second_raw.append(sublanes(turned, row_cell))
-
-    lat_mask[pl.ds(8, 8)] = jnp.where(below[10] > 0.0, 1.0, 0.0)
-    lat_mask[pl.ds(48, 8)] = jnp.where(upper[10] > 0.0, 1.0, 0.0)
-    for ch in range(CHANNELS):
-        lat_field[ch, pl.ds(8, 8)] = below[ch]
-        lat_field[ch, pl.ds(48, 8)] = upper[ch]
-    lat_planes[12, pl.ds(8, 8)] = below[10]
-    lat_planes[12, pl.ds(48, 8)] = upper[10]
-    highest = [lat_packs[1, k] for k in range(SENT)]
-    for at, tiles in ((8, below), (40, highest), (48, upper)):
-        sea = lat_mask[pl.ds(at, 8)]
-        opened = (sea * pltpu.roll(sea, LANES - 1, 1), sea * lat_mask[pl.ds(at + 1, 8)])
-        for level in range(2):
-            for way in range(2):
-                found = face_coefficients(
-                    tiles[4 + 2 * way + level], tiles[8 + way], tiles[11 + way], opened[way]
-                )
-                for j in range(3):
-                    lat_planes[6 * level + 3 * way + j, pl.ds(at, 8)] = found[j]
-
-    opened = lat_mask[pl.ds(47, 8)] * lat_mask[pl.ds(48, 8)]
-    for level in range(2):
-        found = face_coefficients(second_raw[level], second_raw[2], second_raw[3], opened)
-        for j in range(3):
-            lat_second[3 * level + j] = jnp.where(top, found[j], lat_planes[6 * level + 3 + j, pl.ds(47, 8)])
-
-    lat_pair, lon_pair = (lat_field, lat_guess), (lon_field, lon_guess)
-
-    def lat_units(k, results):
-        return [
-            unit(
-                lat_pair[k % 2],
-                lat_pair[(k + 1) % 2],
-                lat_field if k % 2 else None,
-                lat_planes,
-                lat_flux,
-                ch,
-                2,
-                start,
-                count,
-                (lat_second, 48),
-                None,
-                results,
-            )
-            for ch in range(CHANNELS)
-            for start, count in (((8, 48),) if k < 2 * STEPS - 1 else ((8, 16), (32, 16)))
-        ]
-
-    def lon_units(k):
-        def patch(result, rows):
-            n = result.shape[0]
-            return jnp.where(patch_lanes(n), patches[k, pl.ds(rows.start - 8, n)], result)
-
-        return [
-            unit(
-                lon_pair[k % 2],
-                lon_pair[(k + 1) % 2],
-                lon_field if k % 2 else None,
-                lon_planes,
-                lon_flux,
-                0,
-                1,
-                8 + r,
-                min(GROUP, ROWS + 16 - r),
-                (lon_second, ROWS + 16),
-                None if k == 2 * STEPS - 1 else patch,
-                [],
-            )
-            for r in range(0, ROWS + 16, GROUP)
-        ]
-
-    def lat_done(k, results):
-        if k < 2 * STEPS - 1:
-            for at, to in ((0, 0), (32, ROWS)):
-                patches[k, pl.ds(to, 16)] = patch_of([r[at : at + 16] for r in results])
-        else:
-            for ch in range(CHANNELS):
-                field[ch, pl.ds(8, 8)] = lat_field[ch, pl.ds(16, 8)]
-                field[ch, pl.ds(ROWS, 8)] = lat_field[ch, pl.ds(40, 8)]
-
-    for k in range(2 * STEPS):
-        results = []
-        pipeline(lat_units(k, results))
-        lat_done(k, results)
-
-    @pl.when(jnp.logical_not(bottom))
-    def _():
-        for side in range(2):
-            remote(
-                edges.at[side, pl.ds(0, 8)],
-                edges.at[side, pl.ds(0, 8)],
-                corner_send.at[0],
-                corner_recv.at[side],
-                lon,
-                lat,
-            ).wait_recv()
-
-    @pl.when(jnp.logical_not(self_left))
-    def _():
-        remote(
-            edges.at[0, pl.ds(ROWS + 8, 8)],
-            edges.at[0, pl.ds(ROWS + 8, 8)],
-            corner_send.at[0],
-            corner_recv.at[2],
-            lon,
-            lat,
-        ).wait_recv()
-
-    @pl.when(jnp.logical_not(self_right))
-    def _():
-        remote(
-            edges.at[1, pl.ds(ROWS + 8, 8)],
-            edges.at[1, pl.ds(ROWS + 8, 8)],
-            corner_send.at[0],
-            corner_recv.at[3],
-            lon,
-            lat,
-        ).wait_recv()
-
-    for side in range(2):
-        remote(
-            edges.at[side, pl.ds(8, ROWS)],
-            edges.at[side, pl.ds(8, ROWS)],
-            lon_send.at[0],
-            lon_recv.at[side],
-            lon,
-            lat,
-        ).wait_recv()
+    @pl.when(early)
+    def _():
+        dispatch()
 
     half = lane & 64
     far_index = [half + 16 * (j + level_lane) + 8 + place for j in (0, 2)]
@@ -665,29 +524,6 @@
         if a in (0, 2, 5):
             return (spot & 15) >= jnp.where(spot < 64, 8, 7)
         return (spot & 15) >= 8
-
-    cell, raw = own_strips(below[:4], below[4:8], below[8:])
-    lon_field[0, pl.ds(8, 8)] = cell
-    for a, strip in enumerate(raw):
-        lon_raw[a, pl.ds(0, 8)] = strip
-
-    cell, raw = own_strips(across[:4], across[4:8], across[8:])
-    corners = [edges[side, pl.ds(ROWS + 8, 8)] for side in range(2)]
-    far_cell, far_raw = far_strips(
-        jnp.where(top, corners[1], corners[0]), jnp.where(top, corners[0], corners[1])
-    )
-    side_swap = jnp.where(top, lane ^ 64, lane)
-    cell = lanes(jnp.where(own_lanes(8, 1), cell, far_cell), side_swap)
-    lon_field[0, pl.ds(ROWS + 16, 8)] = sublanes(cell, row_cell)
-    second_raw = []
-    for a in range(8):
-        strip = raw[a] if a == 7 else jnp.where(own_lanes(8, a), raw[a], far_raw[a])
-        turned = lanes(strip, side_swap)
-        if a == 1:
-            turned = turned * sign
-        lon_raw[a, pl.ds(ROWS + 8, 8)] = sublanes(turned, row_north if a in (1, 3, 6) else row_cell)
-        if a in (1, 3, 6):
-            second_raw.append(sublanes(turned, row_cell))
 
     def join(r, n):
         rows, padded = pl.ds(r, n), pl.ds(r + 8, n)
@@ -718,8 +554,196 @@
         for j in range(6):
             lon_planes[j, padded] = found[j]
 
-    for r in range(0, ROWS + 16, JOIN):
-        join(r, JOIN)
+    columns_first = jnp.logical_or(lon == 1, jnp.logical_not(jnp.logical_or(top, lat == lat_count // 2)))
+
+    def columns():
+        for side in range(2):
+            remote(
+                edges.at[side, pl.ds(8, ROWS)],
+                edges.at[side, pl.ds(8, ROWS)],
+                lon_send.at[0],
+                lon_recv.at[side],
+                lon,
+                lat,
+            ).wait_recv()
+
+        join(8, 128)
+        join(136, ROWS - 136)
+
+    @pl.when(columns_first)
+    def _():
+        columns()
+
+    remote(lat_edges.at[1], lat_edges.at[1], lat_send.at[0], lat_recv.at[1], lon, lat).wait_recv()
+
+    @pl.when(jnp.logical_not(bottom))
+    def _():
+        remote(lat_edges.at[0], lat_edges.at[0], lat_send.at[0], lat_recv.at[0], lon, lat).wait_recv()
+
+    below = [lat_edges[0, k] for k in range(SENT)]
+    across = [lat_edges[1, k] for k in range(SENT)]
+    norths = (6, 7, 9, 12)
+    row_cell = jnp.where(top, 7 - row8, row8)
+    row_north = jnp.where(top, jnp.maximum(6 - row8, 0), row8)
+    sign = jnp.where(top, -1.0, 1.0)
+    lane_cell = jnp.where(top, LANES - 1 - lane, lane)
+    lane_east = jnp.where(top, jnp.maximum(LANES - 2 - lane, 0), lane)
+    upper, second_raw = [], []
+    for k in range(SENT):
+        turned = lanes(across[k], lane_east if k in (4, 5, 8, 11) else lane_cell)
+        if k in (4, 5, 6, 7):
+            turned = turned * sign
+        upper.append(sublanes(turned, row_north if k in norths else row_cell))
+        if k in norths:
+            second_raw.append(sublanes(turned, row_cell))
+
+    lat_mask[pl.ds(8, 8)] = jnp.where(below[10] > 0.0, 1.0, 0.0)
+    lat_mask[pl.ds(48, 8)] = jnp.where(upper[10] > 0.0, 1.0, 0.0)
+    for ch in range(CHANNELS):
+        lat_field[ch, pl.ds(8, 8)] = below[ch]
+        lat_field[ch, pl.ds(48, 8)] = upper[ch]
+    lat_planes[12, pl.ds(8, 8)] = below[10]
+    lat_planes[12, pl.ds(48, 8)] = upper[10]
+    highest = [lat_packs[1, k] for k in range(SENT)]
+    for at, tiles in ((8, below), (40, highest), (48, upper)):
+        sea = lat_mask[pl.ds(at, 8)]
+        opened = (sea * pltpu.roll(sea, LANES - 1, 1), sea * lat_mask[pl.ds(at + 1, 8)])
+        for level in range(2):
+            for way in range(2):
+                found = face_coefficients(
+                    tiles[4 + 2 * way + level], tiles[8 + way], tiles[11 + way], opened[way]
+                )
+                for j in range(3):
+                    lat_planes[6 * level + 3 * way + j, pl.ds(at, 8)] = found[j]
+
+    opened = lat_mask[pl.ds(47, 8)] * lat_mask[pl.ds(48, 8)]
+    for level in range(2):
+        found = face_coefficients(second_raw[level], second_raw[2], second_raw[3], opened)
+        for j in range(3):
+            lat_second[3 * level + j] = jnp.where(top, found[j], lat_planes[6 * level + 3 + j, pl.ds(47, 8)])
+
+    lat_pair, lon_pair = (lat_field, lat_guess), (lon_field, lon_guess)
+
+    def lat_units(k, results):
+        return [
+            unit(
+                lat_pair[k % 2],
+                lat_pair[(k + 1) % 2],
+                lat_field if k % 2 else None,
+                lat_planes,
+                lat_flux,
+                ch,
+                2,
+                start,
+                count,
+                (lat_second, 48),
+                None,
+                results,
+            )
+            for ch in range(CHANNELS)
+            for start, count in (((8, 48),) if k < 2 * STEPS - 1 else ((8, 16), (32, 16)))
+        ]
+
+    def lon_units(k):
+        def patch(result, rows):
+            n = result.shape[0]
+            return jnp.where(patch_lanes(n), patches[k, pl.ds(rows.start - 8, n)], result)
+
+        return [
+            unit(
+                lon_pair[k % 2],
+                lon_pair[(k + 1) % 2],
+                lon_field if k % 2 else None,
+                lon_planes,
+                lon_flux,
+                0,
+                1,
+                8 + r,
+                min(GROUP, ROWS + 16 - r),
+                (lon_second, ROWS + 16),
+                None if k == 2 * STEPS - 1 else patch,
+                [],
+            )
+            for r in range(0, ROWS + 16, GROUP)
+        ]
+
+    def lat_done(k, results):
+        if k < 2 * STEPS - 1:
+            for at, to in ((0, 0), (32, ROWS)):
+                patches[k, pl.ds(to, 16)] = patch_of([r[at : at + 16] for r in results])
+        else:
+            for ch in range(CHANNELS):
+                field[ch, pl.ds(8, 8)] = lat_field[ch, pl.ds(16, 8)]
+                field[ch, pl.ds(ROWS, 8)] = lat_field[ch, pl.ds(40, 8)]
+
+    for k in range(2 * STEPS):
+        results = []
+        pipeline(lat_units(k, results))
+        lat_done(k, results)
+
+    @pl.when(jnp.logical_not(columns_first))
+    def _():
+        columns()
+
+    @pl.when(jnp.logical_not(bottom))
+    def _():
+        for side in range(2):
+            remote(
+                edges.at[side, pl.ds(0, 8)],
+                edges.at[side, pl.ds(0, 8)],
+                corner_send.at[0],
+                corner_recv.at[side],
+                lon,
+                lat,
+            ).wait_recv()
+
+    @pl.when(jnp.logical_not(self_left))
+    def _():
+        remote(
+            edges.at[0, pl.ds(ROWS + 8, 8)],
+            edges.at[0, pl.ds(ROWS + 8, 8)],
+            corner_send.at[0],
+            corner_recv.at[2],
+            lon,
+            lat,
+        ).wait_recv()
+
+    @pl.when(jnp.logical_not(self_right))
+    def _():
+        remote(
+            edges.at[1, pl.ds(ROWS + 8, 8)],
+            edges.at[1, pl.ds(ROWS + 8, 8)],
+            corner_send.at[0],
+            corner_recv.at[3],
+            lon,
+            lat,
+        ).wait_recv()
+
+    cell, raw = own_strips(below[:4], below[4:8], below[8:])
+    lon_field[0, pl.ds(8, 8)] = cell
+    for a, strip in enumerate(raw):
+        lon_raw[a, pl.ds(0, 8)] = strip
+
+    cell, raw = own_strips(across[:4], across[4:8], across[8:])
+    corners = [edges[side, pl.ds(ROWS + 8, 8)] for side in range(2)]
+    far_cell, far_raw = far_strips(
+        jnp.where(top, corners[1], corners[0]), jnp.where(top, corners[0], corners[1])
+    )
+    side_swap = jnp.where(top, lane ^ 64, lane)
+    cell = lanes(jnp.where(own_lanes(8, 1), cell, far_cell), side_swap)
+    lon_field[0, pl.ds(ROWS + 16, 8)] = sublanes(cell, row_cell)
+    second_raw = []
+    for a in range(8):
+        strip = raw[a] if a == 7 else jnp.where(own_lanes(8, a), raw[a], far_raw[a])
+        turned = lanes(strip, side_swap)
+        if a == 1:
+            turned = turned * sign
+        lon_raw[a, pl.ds(ROWS + 8, 8)] = sublanes(turned, row_north if a in (1, 3, 6) else row_cell)
+        if a in (1, 3, 6):
+            second_raw.append(sublanes(turned, row_cell))
+
+    join(0, 8)
+    join(ROWS, 16)
 
     seas = [jnp.where(lon_planes[6, pl.ds(ROWS + 15 + i, 8)] > 0.0, 1.0, 0.0) for i in range(2)]
     found = face_coefficients(*second_raw, seas[0] * seas[1])

time: 16.4 us -> 16.1 us (0.982); the launches traced: 16.1 us -> 16 us
  no operation moved by 1% of the time
where the time goes in v4:
time: 16.1 us; the launch traced here: 16 us
  Pallas kernels  15.2 us (94%)
  local copies, waits for them, and re-layouts  0.8 us (5%)
    pallas_call x1, Pallas kernels, local(): pl.pallas_call(functools.partial(kernel, lon_count, lat_count), out_shape...  15.2 us
    unnamed x1, local copies, waits for them, and re-layouts  0.8 us

profile of v4, /device:TPU:4, one launch (start us, length us, event | category | flops | bytes accessed | tf_op | source)
XLA Modules:
  0.0 16.0 jit_solution(10709771981538971682)
XLA Ops:
  0.0 15.2 %shard_map.64 = f32[2,2,256,128]{3,2,1,0:T(8,128)S(1)} custom-call(f32[2,2,256,128]{3,2,1,0:T(8,128)} %tracer.1, f32[2,2,256,128]{3,2,1,0:T(8,128)} %transport.1, f32[2,256,128]{2,1,0:T(8,128)} %diffusion.1, f32[256,128]{1,0:T(8,128)} %inverse_volume.1, s32[256,128]{1,0:T(8,128)} %sea_mask.1, s32[2,256,128]{2,1,0:T(8,128)} %regime.1), custom_call_target="tpu_custom_call" | custom-call | tf_op jit(solution)/shard_map/pallas_call | solution.py:805
  15.2 0.8 %copy.8 = f32[2,2,256,128]{3,2,1,0:T(8,128)} copy(f32[2,2,256,128]{3,2,1,0:T(8,128)S(1)} %shard_map.64) | data formatting | bytes 1048576

commit v5 on v4

--- a/solution.py
+++ b/solution.py
@@ -622,6 +622,13 @@
         for j in range(3):
             lat_second[3 * level + j] = jnp.where(top, found[j], lat_planes[6 * level + 3 + j, pl.ds(47, 8)])
 
+    cell, raw = own_strips(below[:4], below[4:8], below[8:])
+    lon_field[0, pl.ds(8, 8)] = cell
+    for a, strip in enumerate(raw):
+        lon_raw[a, pl.ds(0, 8)] = strip
+
+    own_across = own_strips(across[:4], across[4:8], across[8:])
+
     lat_pair, lon_pair = (lat_field, lat_guess), (lon_field, lon_guess)
 
     def lat_units(k, results):
@@ -719,12 +726,7 @@
             lat,
         ).wait_recv()
 
-    cell, raw = own_strips(below[:4], below[4:8], below[8:])
-    lon_field[0, pl.ds(8, 8)] = cell
-    for a, strip in enumerate(raw):
-        lon_raw[a, pl.ds(0, 8)] = strip
-
-    cell, raw = own_strips(across[:4], across[4:8], across[8:])
+    cell, raw = own_across
     corners = [edges[side, pl.ds(ROWS + 8, 8)] for side in range(2)]
     far_cell, far_raw = far_strips(
         jnp.where(top, corners[1], corners[0]), jnp.where(top, corners[0], corners[1])

time: 16.1 us -> 16.1 us (level)
  no operation moved by 1% of the time
where the time goes in v5:
time: 16.1 us; the launch traced here: 16 us
  Pallas kernels  15.2 us (94%)
  local copies, waits for them, and re-layouts  0.8 us (5%)
    pallas_call x1, Pallas kernels, local(): pl.pallas_call(functools.partial(kernel, lon_count, lat_count), out_shape...  15.2 us
    unnamed x1, local copies, waits for them, and re-layouts  0.8 us

profile of v5, /device:TPU:4, one launch (start us, length us, event | category | flops | bytes accessed | tf_op | source)
XLA Modules:
  0.0 16.0 jit_solution(13804001553254389851)
XLA Ops:
  0.0 15.2 %shard_map.64 = f32[2,2,256,128]{3,2,1,0:T(8,128)S(1)} custom-call(f32[2,2,256,128]{3,2,1,0:T(8,128)} %tracer.1, f32[2,2,256,128]{3,2,1,0:T(8,128)} %transport.1, f32[2,256,128]{2,1,0:T(8,128)} %diffusion.1, f32[256,128]{1,0:T(8,128)} %inverse_volume.1, s32[256,128]{1,0:T(8,128)} %sea_mask.1, s32[2,256,128]{2,1,0:T(8,128)} %regime.1), custom_call_target="tpu_custom_call" | custom-call | tf_op jit(solution)/shard_map/pallas_call | solution.py:807
  15.2 0.8 %copy.8 = f32[2,2,256,128]{3,2,1,0:T(8,128)} copy(f32[2,2,256,128]{3,2,1,0:T(8,128)S(1)} %shard_map.64) | data formatting | bytes 1048576
